TPU v7x, 32 devices: a whole 2x2x4 slice. The times are simulated.
32 devices in a mesh: grp: 2 (over core), aux: 4 (over y, x), orb: 4 (over z).
Axes of the slice: x: 2, y: 2, z: 4, core: 2. Of those that a mesh axis runs over, the one named last changes fastest.
Arguments:
- fitted_tensor: bfloat16 [4, 8192, 8192], P('grp', 'aux', 'orb'), may hold values from -0.23925781 to 0.23925781
- block_mask: int32 [2, 64, 64], P('grp'), may hold values 0 or 1
- orbitals: bfloat16 [8192, 256], P('aux'), may hold values from -0.0625 to 0.0625
- nuclear: float32 [8192], replicated, may hold values from 0.5 to 1.5
- centres: float32 [3, 8192], replicated, may hold values from 0 to 8
- mm_positions: float32 [3, 32768], P(None, ('grp', 'aux', 'orb')), may hold values from 0 to 8
- mm_charges: float32 [32768], P(('grp', 'aux', 'orb')), may hold values from -0.12 to 0.12
- neighbours: int32 [32, 2], P(('grp', 'aux', 'orb')), may hold values from 0 to 63, all different within a row
Outputs:
- fock: float32 [8192, 8192], P(('aux', 'orb'))
- mm_potential: float32 [32768], P(('grp', 'aux', 'orb'))
Inputs may be any that keep to these rules, and one draw needn't show every extreme that they name: `neighbours`: each row names 2 different blocks; every block is named by some row.
All inputs are finite; a program needn't handle non-finite values. No bound on the sum of `block_mask` on one device may be relied on, other than what follows from the above.
Results may differ from a plain program's by a relative error of at most 0.01.
Values may be sent and summed in bfloat16 or wider, within the bound.
A program may use at most 128 MiB of HBM per device.

v0:
```python
import jax
import jax.numpy as jnp
from jax import lax
from jax.sharding import PartitionSpec as P

BLK = 128


softening = 1.0


def near_kernel(picker, centre_blocks, charge_blocks, atom_xyz):
    near_xyz = jnp.einsum("kb,cbj->ckj", picker, centre_blocks, precision=lax.Precision.HIGHEST)
    near_xyz = near_xyz.reshape(3, picker.shape[0] * centre_blocks.shape[2])
    near_q = jnp.dot(picker, charge_blocks, precision=lax.Precision.HIGHEST).reshape(-1)
    offsets = near_xyz[:, :, None] - atom_xyz[:, None, :]
    kernel = lax.rsqrt(jnp.sum(offsets * offsets, axis=0) + softening)
    return (kernel, near_q)


def add_diagonal(fock_rows, first_row, field_vec):
    row_count = fock_rows.shape[0]
    values = lax.dynamic_slice_in_dim(field_vec, first_row, row_count, 0)
    row_ids = jnp.arange(row_count, dtype=jnp.int32)[:, None]
    col_ids = jnp.arange(fock_rows.shape[1], dtype=jnp.int32)[None, :]
    on_diagonal = col_ids == first_row + row_ids
    return fock_rows + jnp.where(on_diagonal, values[:, None], jnp.float32(0.0))


def block_picker(first, count, block_total):
    positions = (first + jnp.arange(count, dtype=jnp.int32)) // BLK
    block_ids = jnp.arange(block_total, dtype=jnp.int32)
    return (positions[:, None] == block_ids[None, :]).astype(jnp.float32)


def per_device(
    fitted_tensor, block_mask, orbitals, nuclear, centres, mm_positions, mm_charges, neighbours
):
    row_span = fitted_tensor.shape[1]
    col_span = fitted_tensor.shape[2]
    orb_count = lax.axis_size("orb")
    aux_id = lax.axis_index("aux")
    orb_id = lax.axis_index("orb")
    own_span = row_span // orb_count
    block_total = block_mask.shape[1]
    whole_c = lax.all_gather(orbitals, "aux", axis=0, tiled=True)
    row_start = aux_id * row_span
    col_start = orb_id * col_span
    window_c = lax.dynamic_slice_in_dim(whole_c, col_start, col_span, 0)
    row_pick = block_picker(row_start, row_span, block_total)
    col_pick = block_picker(col_start, col_span, block_total)
    row_bits = jnp.dot(row_pick, block_mask[0].astype(jnp.float32), precision=lax.Precision.HIGHEST)
    mask_wide = jnp.dot(row_bits, col_pick.T, precision=lax.Precision.HIGHEST).astype(jnp.bfloat16)
    masked = fitted_tensor * mask_wide[None]
    x_partial = jnp.einsum("pmn,ni->pmi", masked, window_c, preferred_element_type=jnp.float32)
    x_rows = lax.psum(x_partial, "orb")
    own_rows = lax.dynamic_slice_in_dim(x_rows, orb_id * own_span, own_span, 1)
    x_own = own_rows.astype(jnp.bfloat16)
    own_c = lax.dynamic_slice_in_dim(orbitals, orb_id * own_span, own_span, 0)
    dens_part = 2.0 * jnp.einsum("pmi,mi->p", x_own, own_c, preferred_element_type=jnp.float32)
    densities = lax.psum(dens_part, ("aux", "orb")).astype(jnp.bfloat16)
    coulomb_block = jnp.einsum("pmn,p->mn", masked, densities, preferred_element_type=jnp.float32)
    coulomb = lax.all_to_all(coulomb_block, "orb", split_axis=0, concat_axis=1, tiled=True)
    c_float = whole_c.astype(jnp.float32)
    population = 2.0 * jnp.sum(c_float * c_float, axis=1)
    qm_charge = nuclear - population
    centre_blocks = centres.reshape(3, block_total, BLK)
    charge_blocks = qm_charge.reshape(block_total, BLK)
    picker = (neighbours[0][:, None] == jnp.arange(block_total, dtype=jnp.int32)[None, :]).astype(
        jnp.float32
    )
    kernel, near_q = near_kernel(picker, centre_blocks, charge_blocks, mm_positions)
    mm_potential = jnp.dot(near_q, kernel, precision=lax.Precision.HIGHEST)
    contrib = jnp.dot(kernel, mm_charges, precision=lax.Precision.HIGHEST).reshape(
        picker.shape[0], BLK
    )
    field_part = jnp.dot(picker.T, contrib, precision=lax.Precision.HIGHEST)
    field_sum = lax.psum(field_part, ("grp", "aux", "orb"))
    field_vec = field_sum.reshape(-1)
    own_first = row_start + orb_id * own_span
    exchange_part = jnp.einsum(
        "pmi,pni->mn",
        x_own,
        lax.all_gather(x_own, ("aux", "orb"), axis=1, tiled=True),
        preferred_element_type=jnp.float32,
    )
    fock_part = coulomb - 0.5 * exchange_part
    fock_sum = lax.psum(fock_part, "grp")
    fock = add_diagonal(fock_sum, own_first, field_vec)
    return (fock, mm_potential)


def solution(mesh):
    in_specs = (
        P("grp", "aux", "orb"),
        P("grp", None, None),
        P("aux", None),
        P(),
        P(),
        P(None, ("grp", "aux", "orb")),
        P(("grp", "aux", "orb")),
        P(("grp", "aux", "orb"), None),
    )
    out_specs = (P(("aux", "orb"), None), P(("grp", "aux", "orb")))
    return jax.shard_map(
        per_device, mesh=mesh, in_specs=in_specs, out_specs=out_specs, check_vma=False
    )
```

profile of v0, /device:TPU:0, one launch (start us, length us, event | category | flops | bytes accessed | tf_op | source)
XLA Modules:
  0.0 848.3 jit_solution(9946186388667584154)
XLA Ops:
  7.2 0.0 copy-start
  7.2 0.0 all-gather.3.cloned.1.call-start
  7.2 0.7 all-gather.3.cloned.1.call-update
  8.0 1.0 bitcast_convert_fusion
  9.0 1.7 fusion.6
  10.6 7.5 convolution_convert_fusion
  18.1 14.8 %broadcast_multiply_fusion = bf16[2,2048,2048]{2,1,0:T(8,128)(2,1)} fusion(bf16[2,2048,2048]{2,1,0:T(8,128)(2,1)} %param.8, bf16[2048,2048]{1,0:T(8,128)(2,1)S(1)} %convolution_convert_fusion), kind=kLoop, calls=%fused_computation.7 | loop fusion | flops 8388608 | bytes 41943040 | tf_op jit(solution)/shard_map/mul | solution.py:54
  32.9 32.4 %all-gather.3.cloned.1.call-done = bf16[8192,256]{1,0:T(8,128)(2,1)} async-done(((bf16[2048,256]{1,0:T(8,128)(2,1)}), bf16[8192,256]{1,0:T(8,128)(2,1)}) %all-gather.3.cloned.1.call-update) | async-done | bytes 4194320 | tf_op jit(solution)/shard_map/all_gather | solution.py:46
  65.3 12.5 %fusion.3 = f32[2,2048,256]{2,1,0:T(8,128)} fusion(bf16[2,2048,2048]{2,1,0:T(8,128)(2,1)} %broadcast_multiply_fusion, bf16[8192,256]{1,0:T(8,128)(2,1)} %all-gather.3.cloned.1.call-done, s32[]{:T(128)S(6)} %select_n.32), kind=kOutput, calls=%fused_computation.12 | convolution fusion | flops 4294967296 | bytes 22020100 | tf_op jit(solution)/shard_map/pmn,ni->pmi/dot_general | solution.py:55
  77.8 147.1 %all-reduce.4 = bf16[2,2048,256]{2,1,0:T(8,128)(2,1)S(1)} all-reduce(f32[2,2048,256]{2,1,0:T(8,128)} %fusion.3), channel_id=1, replica_groups=mesh['grp'=2,'aux'=4,'orb'=4] {'orb'}, use_global_device_ids=true, to_apply=%region_0.1 | all-reduce | flops 1048576 | bytes 6291456 | tf_op jit(solution)/shard_map/psum | solution.py:56
  224.9 1.0 multiply_reduce_fusion.2
  225.9 38.2 %psum.29 = bf16[2]{0:T(256)(128)(2,1)S(1)} all-reduce(f32[2]{0:T(128)S(1)} %broadcast_multiply_fusion.1), channel_id=1, replica_groups=mesh['grp'=2,'aux'=4,'orb'=4] {'aux','orb'}, use_global_device_ids=true, to_apply=%region_1.2 | all-reduce | flops 2 | bytes 12 | tf_op jit(solution)/shard_map/psum | solution.py:61
  264.2 28.8 %fusion.1 = f32[1,2048,2048]{2,0,1:T(1,128)S(1)} fusion(bf16[2,2048,2048]{2,1,0:T(8,128)(2,1)} %broadcast_multiply_fusion, bf16[2]{0:T(256)(128)(2,1)S(1)} %psum.29), kind=kOutput, calls=%fused_computation.4 | convolution fusion | flops 16777216 | bytes 33554436 | tf_op jit(solution)/shard_map/pmn,p->mn/dot_general | solution.py:62
  292.9 11.3 %copy.18 = f32[1,2048,2048]{2,1,0:T(8,128)} copy(f32[1,2048,2048]{2,0,1:T(1,128)S(1)} %fusion.1) | data formatting | bytes 33554432 | tf_op jit(solution)/shard_map/pmn,p->mn/dot_general | solution.py:62
  304.2 7.0 all-to-all-start
  311.2 0.0 all-gather.5.cloned.1.call-start
  311.2 0.7 all-gather.5.cloned.1.call-update
  312.0 0.0 all-reduce.3.cloned.1.call-start
  312.0 433.2 %all-to-all-done = f32[4,512,2048]{2,1,0:T(8,128)} async-done(((f32[4,512,2048]{2,1,0:T(8,128)}), f32[4,512,2048]{2,1,0:T(8,128)}, u32[]{:S(2)}, u32[]{:S(2)}) %all-to-all-start) | async-done | bytes 16777248 | tf_op jit(solution)/shard_map/all_to_all | solution.py:63
  745.2 0.0 copy-start.1
  745.2 11.9 %copy.21 = f32[4,64,8,2048]{3,2,0,1:T(8,128)} copy(f32[4,64,8,2048]{3,2,1,0:T(8,128)} %bitcast.23) | data formatting | bytes 33554432 | tf_op jit(solution)/shard_map/all_to_all | solution.py:63
  757.0 0.0 all-gather.5.cloned.1.call-done
  757.0 0.0 copy-done.1
  757.0 14.4 %fusion = f32[512,8192]{1,0:T(8,128)} fusion(f32[512,8192]{1,0:T(8,128)} %bitcast.59, bf16[2,512,256]{2,1,0:T(8,128)(2,1)S(1)} %copy-done.1, bf16[2,8192,256]{2,1,0:T(8,128)(2,1)} %all-gather.5.cloned.1.call-done), kind=kOutput, calls=%fused_computation.1 | convolution fusion | flops 4303355904 | bytes 42467328 | tf_op jit(solution)/shard_map/pmi,pni->mn/dot_general | solution.py:81
  771.4 0.0 copy-start.2
  771.4 0.0 copy-start.5
  771.4 0.0 copy-start.4
  771.4 0.0 copy-start.3
  771.5 0.0 all-reduce.3.cloned.1.call-update
  771.5 0.9 copy-done.2
  772.3 0.0 copy-done.5
  772.3 0.2 convolution_bitcast_fusion.1
  772.5 0.0 copy-done.4
  772.5 0.4 multiply_reduce_fusion.1
  772.9 0.0 copy-done
  772.9 1.0 fusion.8
  773.9 0.3 convolution_bitcast_fusion
  774.2 37.3 %psum.31 = f32[8192]{0:T(1024)S(1)} all-reduce(f32[8192]{0:T(1024)S(1)} %convolution_bitcast_fusion), channel_id=1, replica_groups=mesh['grp'=2,'aux'=4,'orb'=4] {'grp','aux','orb'}, use_global_device_ids=true, to_apply=%region_4.5 | all-reduce | flops 8192 | bytes 65536 | tf_op jit(solution)/shard_map/psum | solution.py:78
  811.5 0.1 dynamic_slice.15
  811.6 3.8 multiply_reduce_fusion
  815.3 0.0 copy-done.3
  815.3 0.2 fusion.15
  815.5 1.3 fusion.7
  816.8 12.9 %all-reduce.3.cloned.1.call-done = f32[512,8192]{1,0:T(8,128)} async-done(((f32[512,8192]{1,0:T(8,128)}), f32[512,8192]{1,0:T(8,128)}) %all-reduce.3.cloned.1.call-update) | async-done | bytes 16777232 | tf_op jit(solution)/shard_map/psum | solution.py:88
  829.7 12.1 %select_add_fusion = f32[512,8192]{1,0:T(8,128)} fusion(f32[512,8192]{1,0:T(8,128)} %all-reduce.3.cloned.1.call-done, f32[512]{0:T(512)S(1)} %dynamic_slice.15, s32[512]{0:T(512)S(1)} %iota_add_fusion.2), kind=kLoop, calls=%fused_computation.2 | loop fusion | flops 12582912 | bytes 33558528 | tf_op jit(solution)/shard_map/add | solution.py:27
  (5 shorter events, 0.0 us)
Async XLA Ops:
  7.2 765.8 %copy-start = (f32[1024]{0:T(1024)S(1)}, f32[1024]{0:T(1024)}, u32[]{:S(2)}) copy-start(f32[1024]{0:T(1024)} %param.14) | copy-start | bytes 12292
  7.2 58.1 %all-gather.3.cloned.1.call-start = ((), (), s32[]{:S(2)}) async-start(), calls=%async_computation.1 | async-start | bytes 5242880 | tf_op jit(solution)/shard_map/all_gather | solution.py:46
  304.2 440.9 %all-to-all-start = ((f32[4,512,2048]{2,1,0:T(8,128)}), f32[4,512,2048]{2,1,0:T(8,128)}, u32[]{:S(2)}, u32[]{:S(2)}) async-start(f32[4,512,2048]{2,1,0:T(8,128)} %bitcast.58), calls=%async_computation | async-start | bytes 33554432 | tf_op jit(solution)/shard_map/all_to_all | solution.py:63
  311.2 445.8 %all-gather.5.cloned.1.call-start = ((), (), s32[]{:S(2)}) async-start(), calls=%async_computation.2 | async-start | bytes 8912896 | tf_op jit(solution)/shard_map/all_gather | solution.py:84
  312.0 517.8 %all-reduce.3.cloned.1.call-start = ((), (), s32[]{:S(2)}) async-start(), calls=%async_computation.3 | async-start | bytes 33554432 | tf_op jit(solution)/shard_map/psum | solution.py:88
  745.2 11.9 %copy-start.1 = (bf16[2,512,256]{2,1,0:T(8,128)(2,1)S(1)}, bf16[2,512,256]{2,1,0:T(8,128)(2,1)}, u32[]{:S(2)}) copy-start(bf16[2,512,256]{2,1,0:T(8,128)(2,1)} %get-tuple-element.3) | copy-start | bytes 1572868
  771.4 0.9 copy-start.2
  771.4 0.9 copy-start.5
  771.4 1.1 copy-start.4
  771.4 43.9 %copy-start.3 = (f32[8192]{0:T(1024)S(1)}, f32[8192]{0:T(1024)}, u32[]{:S(2)}) copy-start(f32[8192]{0:T(1024)} %param.11) | copy-start | bytes 98308
Sparse Core Ops, SparseCore 0:
  9.9 55.3 all-gather.2
  314.8 381.6 all-gather.4
  771.6 58.0 all-reduce.2
where the time goes:
time: 849 us; the launch traced here: 848 us
  waiting for transfers between devices  480 us (57%)
  blocking collectives  223 us (26%)
  matrix products  67.7 us (8%)
  other arithmetic  33.1 us (4%)
  local copies, waits for them, and re-layouts  24.2 us (3%)
  between operations  13.9 us (2%)
    all_to_all x1, waiting for transfers between devices, per_device(): lax.all_to_all(coulomb_block, 'orb', split_axis=0, concat_axis=1, tiled=T...  433 us
    psum x1, blocking collectives, per_device(): x_rows = lax.psum(x_partial, 'orb')  147 us
    psum x1, blocking collectives, per_device(): densities = lax.psum(dens_part, ('aux', 'orb')).astype(jnp.bfloat16)  38.2 us
    psum x1, blocking collectives, per_device(): field_sum = lax.psum(field_part, ('grp', 'aux', 'orb'))  37.3 us
    all_gather x1, waiting for transfers between devices, per_device(): whole_c = lax.all_gather(orbitals, 'aux', axis=0, tiled=True)  32.4 us
    dot_general x1, matrix products, per_device(): jnp.einsum('pmn,p->mn', masked, densities, preferred_element_type=jnp.flo...  28.8 us
  transfers between devices with their start and end apart: 4, of which 3 were waited for; matrix products, arithmetic and copies ran while one was open for 5% of the time, Pallas kernels for 0%

commit v1 on v0

v1 whole, which is shorter than its diff:
```python
import functools

import jax
import jax.numpy as jnp
from jax import lax
from jax.experimental import pallas as pl
from jax.experimental.pallas import tpu as pltpu
from jax.sharding import PartitionSpec as P

BLK = 128
VMEM_LIMIT = 48 * 1024 * 1024

softening = 1.0


def near_kernel(picker, centre_blocks, charge_blocks, atom_xyz):
    near_xyz = jnp.einsum("kb,cbj->ckj", picker, centre_blocks, precision=lax.Precision.HIGHEST)
    near_xyz = near_xyz.reshape(3, picker.shape[0] * centre_blocks.shape[2])
    near_q = jnp.dot(picker, charge_blocks, precision=lax.Precision.HIGHEST).reshape(-1)
    offsets = near_xyz[:, :, None] - atom_xyz[:, None, :]
    kernel = lax.rsqrt(jnp.sum(offsets * offsets, axis=0) + softening)
    return (kernel, near_q)


def products_kernel(t_ref, mask_ref, win_ref, c_ref, x_ref, dens_ref):
    parts, rows, cols = t_ref.shape
    row_mask = mask_ref[0]

    @pl.when(pl.program_id(0) == 0)
    def _():
        dens_ref[...] = jnp.zeros_like(dens_ref)

    own = c_ref[...].astype(jnp.float32)
    for p in range(parts):
        prod = jnp.dot(t_ref[p] * row_mask, win_ref[...], preferred_element_type=jnp.float32)
        x_ref[p] = prod.astype(x_ref.dtype)
        dens_ref[p] += jnp.sum((prod * own).reshape(rows // 8, 8, prod.shape[1]), axis=0)


def products_call(fitted, mask_rows, window_c, own_c):
    parts, rows, cols = fitted.shape
    nocc = window_c.shape[1]
    return pl.pallas_call(
        products_kernel,
        grid=(rows // BLK,),
        in_specs=[
            pl.BlockSpec((parts, BLK, cols), lambda i: (0, i, 0)),
            pl.BlockSpec((1, 1, cols), lambda i: (i, 0, 0)),
            pl.BlockSpec((cols, nocc), lambda i: (0, 0)),
            pl.BlockSpec((BLK, nocc), lambda i: (i, 0)),
        ],
        out_specs=[
            pl.BlockSpec((parts, BLK, nocc), lambda i: (0, i, 0)),
            pl.BlockSpec((parts, 8, nocc), lambda i: (0, 0, 0)),
        ],
        out_shape=[
            jax.ShapeDtypeStruct((parts, rows, nocc), jnp.bfloat16),
            jax.ShapeDtypeStruct((parts, 8, nocc), jnp.float32),
        ],
        compiler_params=pltpu.CompilerParams(vmem_limit_bytes=VMEM_LIMIT),
        cost_estimate=pl.CostEstimate(
            flops=2 * parts * rows * cols * nocc,
            bytes_accessed=2 * parts * rows * (cols + nocc),
            transcendentals=0,
        ),
        name="products",
    )(fitted, mask_rows, window_c, own_c)


def coulomb_kernel(dens_ref, t_ref, mask_ref, out_ref):
    parts = t_ref.shape[0]
    total = t_ref[0].astype(jnp.float32) * dens_ref[0]
    for p in range(1, parts):
        total += t_ref[p].astype(jnp.float32) * dens_ref[p]
    out_ref[...] = (total * mask_ref[0].astype(jnp.float32)).astype(out_ref.dtype)


def coulomb_call(densities, fitted, mask_rows):
    parts, rows, cols = fitted.shape
    return pl.pallas_call(
        coulomb_kernel,
        grid=(rows // BLK,),
        in_specs=[
            pl.BlockSpec(memory_space=pltpu.SMEM),
            pl.BlockSpec((parts, BLK, cols), lambda i: (0, i, 0)),
            pl.BlockSpec((1, 1, cols), lambda i: (i, 0, 0)),
        ],
        out_specs=pl.BlockSpec((BLK, cols), lambda i: (i, 0)),
        out_shape=jax.ShapeDtypeStruct((rows, cols), jnp.bfloat16),
        compiler_params=pltpu.CompilerParams(vmem_limit_bytes=VMEM_LIMIT),
        cost_estimate=pl.CostEstimate(
            flops=2 * parts * rows * cols,
            bytes_accessed=2 * rows * cols * (parts + 1),
            transcendentals=0,
        ),
        name="coulomb",
    )(densities, fitted, mask_rows)


def fock_kernel(place_ref, own_ref, all_ref, coul_ref, field_ref, out_ref):
    parts = own_ref.shape[0]
    rows, cols = out_ref.shape
    half = rows // 2
    dims = (((1,), (1,)), ((), ()))
    total = lax.dot_general(own_ref[0], all_ref[0], dims, preferred_element_type=jnp.float32)
    for p in range(1, parts):
        total += lax.dot_general(own_ref[p], all_ref[p], dims, preferred_element_type=jnp.float32)
    out_ref[...] = -0.5 * total
    first_row = pl.multiple_of(place_ref[0] * half, half)
    out_ref[pl.ds(first_row, half), :] += coul_ref[0].astype(jnp.float32)

    col0 = pl.program_id(0) * cols
    row0 = place_ref[1]

    @pl.when((place_ref[0] == 0) & (row0 < col0 + cols) & (row0 + rows > col0))
    def _():
        row_ids = row0 + lax.broadcasted_iota(jnp.int32, (rows, cols), 0)
        col_ids = col0 + lax.broadcasted_iota(jnp.int32, (rows, cols), 1)
        out_ref[...] += jnp.where(row_ids == col_ids, field_ref[...], jnp.float32(0.0))


def fock_call(place, x_own, x_all, coul, field_col):
    parts, rows, nocc = x_own.shape
    total = x_all.shape[1]
    per_src = coul.shape[2]
    cols = min(1024, per_src)
    step = per_src // cols
    return pl.pallas_call(
        fock_kernel,
        grid=(total // cols,),
        in_specs=[
            pl.BlockSpec(memory_space=pltpu.SMEM),
            pl.BlockSpec((parts, rows, nocc), lambda j: (0, 0, 0)),
            pl.BlockSpec((parts, cols, nocc), lambda j: (0, j, 0)),
            pl.BlockSpec((1, rows // 2, cols), lambda j: (j // step, 0, j % step)),
            pl.BlockSpec((rows, 1), lambda j: (0, 0)),
        ],
        out_specs=pl.BlockSpec((rows, cols), lambda j: (0, j)),
        out_shape=jax.ShapeDtypeStruct((rows, total), jnp.float32),
        compiler_params=pltpu.CompilerParams(vmem_limit_bytes=VMEM_LIMIT),
        cost_estimate=pl.CostEstimate(
            flops=2 * parts * rows * total * nocc,
            bytes_accessed=2 * parts * total * nocc + 4 * rows * total + rows * total,
            transcendentals=0,
        ),
        name="fock",
    )(place, x_own, x_all, coul, field_col)


def per_device(
    fitted_tensor, block_mask, orbitals, nuclear, centres, mm_positions, mm_charges, neighbours
):
    parts, row_span, col_span = fitted_tensor.shape
    nocc = orbitals.shape[1]
    orb_count = lax.axis_size("orb")
    aux_count = lax.axis_size("aux")
    grp_id = lax.axis_index("grp")
    aux_id = lax.axis_index("aux")
    orb_id = lax.axis_index("orb")
    own_span = row_span // orb_count
    half = own_span // 2
    block_total = block_mask.shape[1]
    row_start = aux_id * row_span
    col_start = orb_id * col_span

    if aux_count == orb_count:
        perm = [
            (a * orb_count + o, o * orb_count + a)
            for a in range(aux_count)
            for o in range(orb_count)
        ]
        window_c = lax.ppermute(orbitals, ("aux", "orb"), perm)
    else:
        whole_c = lax.all_gather(orbitals, "aux", axis=0, tiled=True)
        window_c = lax.dynamic_slice_in_dim(whole_c, col_start, col_span, 0)

    bits = lax.dynamic_slice(
        block_mask[0],
        (row_start // BLK, col_start // BLK),
        (row_span // BLK, col_span // BLK),
    ).astype(jnp.bfloat16)
    mask_rows = jnp.repeat(bits, BLK, axis=1)[:, None, :]

    x_part, dens_lanes = products_call(fitted_tensor, mask_rows, window_c, orbitals)
    dens_part = 2.0 * jnp.sum(dens_lanes, axis=(1, 2))
    densities = lax.psum(dens_part, ("aux", "orb")).astype(jnp.bfloat16).astype(jnp.float32)

    x_swap = lax.all_to_all(
        x_part.reshape(parts, orb_count, own_span, nocc), "orb", split_axis=1, concat_axis=1, tiled=True
    )
    x_own = jnp.sum(x_swap.astype(jnp.float32), axis=1).astype(jnp.bfloat16)
    x_all = lax.all_gather(x_own, ("aux", "orb"), axis=1, tiled=True)

    coul = coulomb_call(densities, fitted_tensor, mask_rows)
    coul = coul.reshape(orb_count, 2, half, col_span)
    away = lax.dynamic_index_in_dim(coul, 1 - grp_id, 1, keepdims=False)
    kept = lax.dynamic_index_in_dim(coul, grp_id, 1, keepdims=False)
    got = lax.ppermute(away, "grp", [(0, 1), (1, 0)])
    both = (kept.astype(jnp.float32) + got.astype(jnp.float32)).astype(jnp.bfloat16)
    coul_rows = lax.all_to_all(both, "orb", split_axis=0, concat_axis=0, tiled=True)

    own_float = orbitals.astype(jnp.float32)
    own_population = 2.0 * jnp.sum(own_float * own_float, axis=1)
    population = lax.all_gather(own_population, "aux", axis=0, tiled=True)
    qm_charge = nuclear - population
    centre_blocks = centres.reshape(3, block_total, BLK)
    charge_blocks = qm_charge.reshape(block_total, BLK)
    picker = (neighbours[0][:, None] == jnp.arange(block_total, dtype=jnp.int32)[None, :]).astype(
        jnp.float32
    )
    kernel, near_q = near_kernel(picker, centre_blocks, charge_blocks, mm_positions)
    mm_potential = jnp.dot(near_q, kernel, precision=lax.Precision.HIGHEST)
    contrib = jnp.dot(kernel, mm_charges, precision=lax.Precision.HIGHEST).reshape(
        picker.shape[0], BLK
    )
    field_part = jnp.dot(picker.T, contrib, precision=lax.Precision.HIGHEST)
    field_vec = lax.psum(field_part, ("grp", "aux", "orb")).reshape(-1)

    own_first = row_start + orb_id * own_span
    field_col = lax.dynamic_slice_in_dim(field_vec, own_first, own_span, 0)[:, None]
    place = jnp.stack([grp_id, own_first]).astype(jnp.int32)
    fock_part = fock_call(place, x_own, x_all, coul_rows, field_col)
    fock = lax.psum(fock_part, "grp")
    return (fock, mm_potential)


def solution(mesh):
    in_specs = (
        P("grp", "aux", "orb"),
        P("grp", None, None),
        P("aux", None),
        P(),
        P(),
        P(None, ("grp", "aux", "orb")),
        P(("grp", "aux", "orb")),
        P(("grp", "aux", "orb"), None),
    )
    out_specs = (P(("aux", "orb"), None), P(("grp", "aux", "orb")))
    return jax.shard_map(
        per_device, mesh=mesh, in_specs=in_specs, out_specs=out_specs, check_vma=False
    )
```

time: 849 us -> 465 us (0.55)
  waiting for transfers between devices: 480 us -> 55.5 us
  blocking collectives: 223 us -> 309 us
  matrix products: 67.7 us -> 2.92 us
  Pallas kernels: 0 us -> 45.2 us
  other arithmetic: 33.1 us -> 10.7 us
    all_to_all x1, waiting for transfers between devices: 433 us -> 0.01 us  [per_device(): lax.all_to_all(both, 'orb', split_axis=0, concat_axis=0, tiled=True)]
    all_to_all x0 -> x1, blocking collectives: none -> 120 us  [per_device(): lax.all_to_all(x_part.reshape(parts, orb_count, own_span, nocc), 'orb', s...]
    dot_general x5 -> x0, matrix products: 64.8 us -> none  [the longest x1 28.8 us: per_device(): jnp.einsum('pmn,p->mn', masked, densities, preferred_element_type=jnp.flo...]
    pallas_call x0 -> x3, Pallas kernels: none -> 45.2 us  [the longest x1 15.4 us: coulomb_call(): pl.pallas_call(coulomb_kernel, grid=(rows // BLK,), in_specs=[pl.BlockSpe...]
    psum x3 -> x2, blocking collectives: 223 us -> 180 us  [the longest x1 138 us: per_device(): field_vec = lax.psum(field_part, ('grp', 'aux', 'orb')).reshape(-1)]
    psum x1, waiting for transfers between devices: 12.9 us -> 48 us  [per_device(): fock = lax.psum(fock_part, 'grp')]
    all_gather x2 -> x1, waiting for transfers between devices: 32.4 us -> 0.01 us  [per_device(): x_all = lax.all_gather(x_own, ('aux', 'orb'), axis=1, tiled=True)]
    mul x2, other arithmetic: 14.8 us -> 0.01 us  [the longest x1 0.01 us: per_device(): dens_part = 2.0 * jnp.sum(dens_lanes, axis=(1, 2))]
  transfers between devices with their start and end apart: 4 -> 5, of which waited for: 3 -> 2; matrix products, arithmetic and copies ran while one was open for 5% -> 4% of each run, Pallas kernels for 0% -> 3%
where the time goes in v1:
time: 465 us; the launch traced here: 464 us
  blocking collectives  309 us (66%)
  waiting for transfers between devices  55.5 us (12%)
  Pallas kernels  45.2 us (10%)
  local copies, waits for them, and re-layouts  19.4 us (4%)
  between operations  14.2 us (3%)
  other arithmetic  10.7 us (2%)
  starting transfers between devices  7.05 us (2%)
    psum x1, blocking collectives, per_device(): field_vec = lax.psum(field_part, ('grp', 'aux', 'orb')).reshape(-1)  138 us
    all_to_all x1, blocking collectives, per_device(): lax.all_to_all(x_part.reshape(parts, orb_count, own_span, nocc), 'orb', s...  120 us
    psum x1, waiting for transfers between devices, per_device(): fock = lax.psum(fock_part, 'grp')  48 us
    psum x1, blocking collectives, per_device(): lax.psum(dens_part, ('aux', 'orb')).astype(jnp.bfloat16).astype(jnp.float32)  42 us
    pallas_call x1, Pallas kernels, coulomb_call(): pl.pallas_call(coulomb_kernel, grid=(rows // BLK,), in_specs=[pl.BlockSpe...  15.4 us
    pallas_call x1, Pallas kernels, fock_call(): pl.pallas_call(fock_kernel, grid=(total // cols,), in_specs=[pl.BlockSpec...  15.1 us
    pallas_call x1, Pallas kernels, products_call(): pl.pallas_call(products_kernel, grid=(rows // BLK,), in_specs=[pl.BlockSp...  14.7 us
    unnamed x20, local copies, waits for them, and re-layouts  14.1 us
  transfers between devices with their start and end apart: 5, of which 2 were waited for; matrix products, arithmetic and copies ran while one was open for 4% of the time, Pallas kernels for 3%

profile of v1, /device:TPU:0, one launch (start us, length us, event | category | flops | bytes accessed | tf_op | source)
XLA Modules:
  0.0 463.8 jit_solution(11886421983260858717)
XLA Ops:
  7.2 0.0 copy-start
  7.2 0.0 all-gather.2.cloned.1.call-start
  7.2 1.9 collective-permute-start
  9.1 0.8 fusion.10
  9.9 0.1 broadcast_in_dim.8
  10.0 0.0 collective-permute-done.win_ref
  10.0 0.0 copy-start.3
  10.1 1.2 copy-done.3
  11.3 14.7 %products.1 = (bf16[2,2048,256]{2,1,0:T(8,128)(2,1)S(1)}, f32[2,8,256]{2,1,0:T(8,128)S(1)}) custom-call(bf16[2,2048,2048]{2,1,0:T(8,128)(2,1)} %t_ref.3, bf16[16,1,2048]{2,1,0:T(2,128)(2,1)S(1)} %broadcast_in_dim_reshape.5.mask_ref, bf16[2048,256]{1,0:T(8,128)(2,1)S(1)} %collective-permute-done.win_ref, bf16[2048,256]{1,0:T(8,128)(2,1)S(1)} %copy-done.3), custom_call_target="tpu_custom_call" | custom-call | flops 4294967296 | bytes 18874368 | tf_op jit(solution)/shard_map/products/pallas_call | solution.py:43
  26.0 0.1 copy.20
  26.1 119.6 %all_to_all.10 = bf16[2,4,512,256]{3,2,0,1:T(8,128)(2,1)S(1)} all-to-all(bf16[2,4,512,256]{3,2,0,1:T(8,128)(2,1)S(1)} %copy.20), channel_id=1, replica_groups=mesh['grp'=2,'aux'=4,'orb'=4] {'orb'}, dimensions={1} | all-to-all | bytes 4194304 | tf_op jit(solution)/shard_map/all_to_all | solution.py:188
  145.8 1.2 reduce_sum.39.own_ref
  147.0 0.0 all-gather.2.cloned.1.call-update
  147.0 0.1 reduce_sum.40
  147.1 42.0 %psum.21 = bf16[2]{0:T(256)(128)(2,1)S(1)} all-reduce(f32[2]{0:T(128)S(1)} %broadcast_multiply_fusion.1), channel_id=1, replica_groups=mesh['grp'=2,'aux'=4,'orb'=4] {'aux','orb'}, use_global_device_ids=true, to_apply=%region_2.3 | all-reduce | flops 2 | bytes 12 | tf_op jit(solution)/shard_map/psum | solution.py:186
  189.1 15.4 %coulomb.1 = bf16[2048,2048]{1,0:T(8,128)(2,1)} custom-call(f32[2]{0:T(128)S(1)} %convert_element_type.48.dens_ref, bf16[2,2048,2048]{2,1,0:T(8,128)(2,1)} %t_ref.3, bf16[16,1,2048]{2,1,0:T(2,128)(2,1)S(1)} %broadcast_in_dim_reshape.5.mask_ref), custom_call_target="tpu_custom_call" | custom-call | flops 16777216 | bytes 25165824 | tf_op jit(solution)/shard_map/coulomb/pallas_call | solution.py:80
  204.5 4.7 %dynamic-slice_bitcast_fusion = bf16[4,256,2048]{2,1,0:T(8,128)(2,1)} fusion(bf16[4,2,256,2048]{3,2,1,0:T(8,128)(2,1)} %bitcast.46, s32[]{:T(128)S(6)} %select_n.29), kind=kLoop, calls=%fused_computation.2 | loop fusion | bytes 8388612 | tf_op jit(solution)/shard_map/jit(dynamic_index_in_dim)/squeeze | solution.py:196
  209.2 0.0 collective-permute-start.1
  209.2 7.5 %collective-permute-done.1 = bf16[4,256,2048]{2,1,0:T(8,128)(2,1)} collective-permute-done((bf16[4,256,2048]{2,1,0:T(8,128)(2,1)}, bf16[4,256,2048]{2,1,0:T(8,128)(2,1)}, u32[]{:S(2)}, u32[]{:S(2)}) %collective-permute-start.1) | collective-permute-done | bytes 4194336 | tf_op jit(solution)/shard_map/ppermute | solution.py:198
  216.7 7.8 %fusion = bf16[4,256,2048]{2,1,0:T(8,128)(2,1)} fusion(bf16[4,256,2048]{2,1,0:T(8,128)(2,1)} %collective-permute-done.1, bf16[4,2,256,2048]{3,2,1,0:T(8,128)(2,1)} %bitcast.47, s32[]{:T(128)S(6)} %select_n.28), kind=kLoop, calls=%fused_computation.1 | loop fusion | flops 8388608 | bytes 12582916 | tf_op jit(solution)/shard_map/convert_element_type | solution.py:199
  224.5 0.0 copy-start.5
  224.5 0.0 copy-start.8
  224.5 0.0 copy-start.7
  224.5 0.0 copy-start.2
  224.5 5.1 %all-to-all-start.1 = ((bf16[4,256,2048]{2,1,0:T(8,128)(2,1)}), bf16[4,256,2048]{2,1,0:T(8,128)(2,1)}, u32[]{:S(2)}, u32[]{:S(2)}) async-start(bf16[4,256,2048]{2,1,0:T(8,128)(2,1)} %fusion), calls=%async_computation.1 | async-start | bytes 8388608 | tf_op jit(solution)/shard_map/all_to_all | solution.py:200
  229.6 0.0 all-reduce.2.cloned.1.call-start
  229.6 0.0 copy-done.5
  229.6 0.0 copy-done.8
  229.7 0.2 convolution_bitcast_fusion.1
  229.9 0.0 copy-done.7
  229.9 0.4 multiply_reduce_fusion
  230.2 0.0 copy-done
  230.2 1.0 fusion.2
  231.2 0.3 convolution_bitcast_fusion
  231.5 138.3 %psum.22 = f32[8192]{0:T(1024)S(1)} all-reduce(f32[8192]{0:T(1024)S(1)} %convolution_bitcast_fusion), channel_id=1, replica_groups=mesh['grp'=2,'aux'=4,'orb'=4] {'grp','aux','orb'}, use_global_device_ids=true, to_apply=%region_4.5 | all-reduce | flops 8192 | bytes 65536 | tf_op jit(solution)/shard_map/psum | solution.py:217
  369.8 0.1 dynamic_slice.16
  369.9 0.1 copy.23.field_ref
  370.0 0.1 pad_add_fusion.place_ref
  370.1 0.0 all-to-all-done.1.coul_ref
  370.1 0.0 all-gather.2.cloned.1.call-done.all_ref
  370.1 0.0 copy-done.2
  370.1 15.1 %fock.1 = f32[512,8192]{1,0:T(8,128)} custom-call(s32[2]{0:T(128)S(1)} %pad_add_fusion.place_ref, bf16[2,512,256]{2,1,0:T(8,128)(2,1)S(1)} %copy-done.2, bf16[2,8192,256]{2,1,0:T(8,128)(2,1)} %all-gather.2.cloned.1.call-done.all_ref, bf16[4,256,2048]{2,1,0:T(8,128)(2,1)} %all-to-all-done.1.coul_ref, f32[512,1]{1,0:T(8,128)S(1)} %copy.23.field_ref), custom_call_target="tpu_custom_call" | custom-call | flops 4294967296 | bytes 29360128 | tf_op jit(solution)/shard_map/fock/pallas_call | solution.py:128
  385.3 0.0 copy-start.4
  385.3 0.0 copy-start.6
  385.3 0.0 all-reduce.2.cloned.1.call-update
  385.3 1.2 copy-done.4
  386.5 0.3 multiply_reduce_fusion.1
  386.8 8.9 %all_gather.7 = f32[8192]{0:T(1024)S(1)} all-gather(f32[2048]{0:T(1024)S(1)} %broadcast_multiply_fusion), channel_id=1, replica_groups=mesh['grp'=2,'aux'=4,'orb'=4] {'aux'}, dimensions={0}, use_global_device_ids=true | all-gather | bytes 40960 | tf_op jit(solution)/shard_map/all_gather | solution.py:204
  395.8 0.0 copy-done.6
  395.8 0.2 fusion.7
  396.0 1.3 fusion.1
  397.2 48.0 %all-reduce.2.cloned.1.call-done = f32[512,8192]{1,0:T(8,128)} async-done(((f32[512,8192]{1,0:T(8,128)}), f32[512,8192]{1,0:T(8,128)}) %all-reduce.2.cloned.1.call-update) | async-done | bytes 16777232 | tf_op jit(solution)/shard_map/psum | solution.py:223
  445.2 0.0 copy-start.1
  445.2 11.7 %copy.34 = f32[512,8192]{1,0:T(8,128)} copy(f32[512,8192]{1,0:T(8,128)} %all-reduce.2.cloned.1.call-done) | data formatting | bytes 33554432
  456.9 0.0 copy-done.1
  (5 shorter events, 0.1 us)
Async XLA Ops:
  7.2 223.1 %copy-start = (f32[1024]{0:T(1024)S(1)}, f32[1024]{0:T(1024)}, u32[]{:S(2)}) copy-start(f32[1024]{0:T(1024)} %param.14) | copy-start | bytes 12292
  7.2 362.9 %all-gather.2.cloned.1.call-start = ((), (), s32[]{:S(2)}) async-start(), calls=%async_computation.2 | async-start | bytes 8912896 | tf_op jit(solution)/shard_map/all_gather | solution.py:192
  7.2 2.8 collective-permute-start
  10.0 1.2 copy-start.3
  209.2 7.5 %collective-permute-start.1 = (bf16[4,256,2048]{2,1,0:T(8,128)(2,1)}, bf16[4,256,2048]{2,1,0:T(8,128)(2,1)}, u32[]{:S(2)}, u32[]{:S(2)}) collective-permute-start(bf16[4,256,2048]{2,1,0:T(8,128)(2,1)} %dynamic-slice_bitcast_fusion), channel_id=1, source_target_pairs={{0,16},{16,0},{1,17},{17,1},{2,18},{18,2},{3,19},{19,3},{4,20},{20... | collective-permute-start | bytes 12582920 | tf_op jit(solution)/shard_map/ppermute | solution.py:198
  224.5 5.2 %copy-start.5 = (f32[3,8192]{1,0:T(4,128)S(1)}, f32[3,8192]{1,0:T(4,128)}, u32[]{:S(2)}) copy-start(f32[3,8192]{1,0:T(4,128)} %param.12) | copy-start | bytes 294916
  224.5 5.2 %copy-start.8 = (s32[1,2]{1,0:T(1,128)S(1)}, s32[1,2]{1,0:T(1,128)}, u32[]{:S(2)}) copy-start(s32[1,2]{1,0:T(1,128)} %param.15) | copy-start | bytes 28
  224.5 5.4 %copy-start.7 = (f32[3,1024]{1,0:T(4,128)S(1)}, f32[3,1024]{1,0:T(4,128)}, u32[]{:S(2)}) copy-start(f32[3,1024]{1,0:T(4,128)} %param.13) | copy-start | bytes 36868
  224.5 145.6 %copy-start.2 = (bf16[2,512,256]{2,1,0:T(8,128)(2,1)S(1)}, bf16[2,512,256]{2,1,0:T(8,128)(2,1)}, u32[]{:S(2)}) copy-start(bf16[2,512,256]{2,1,0:T(8,128)(2,1)} %reduce_sum.39.own_ref) | copy-start | bytes 1572868
  224.5 145.6 %all-to-all-start.1 = ((bf16[4,256,2048]{2,1,0:T(8,128)(2,1)}), bf16[4,256,2048]{2,1,0:T(8,128)(2,1)}, u32[]{:S(2)}, u32[]{:S(2)}) async-start(bf16[4,256,2048]{2,1,0:T(8,128)(2,1)} %fusion), calls=%async_computation.1 | async-start | bytes 8388608 | tf_op jit(solution)/shard_map/all_to_all | solution.py:200
  229.6 215.7 %all-reduce.2.cloned.1.call-start = ((), (), s32[]{:S(2)}) async-start(), calls=%async_computation.3 | async-start | bytes 33554432 | tf_op jit(solution)/shard_map/psum | solution.py:223
  385.3 1.2 copy-start.4
  385.3 10.5 %copy-start.6 = (f32[8192]{0:T(1024)S(1)}, f32[8192]{0:T(1024)}, u32[]{:S(2)}) copy-start(f32[8192]{0:T(1024)} %param.11) | copy-start | bytes 98308
  445.2 11.7 %copy-start.1 = (f32[1024]{0:T(1024)S(1)}, f32[1024]{0:T(1024)}, u32[]{:S(2)}) copy-start(f32[1024]{0:T(1024)} %param.14) | copy-start | bytes 12292
Sparse Core Ops, SparseCore 0:
  147.1 148.6 all-gather.1
  385.4 59.7 all-reduce.1

commit v2 on v1

--- a/solution.py
+++ b/solution.py
@@ -67,84 +67,128 @@
     )(fitted, mask_rows, window_c, own_c)
 
 
-def coulomb_kernel(dens_ref, t_ref, mask_ref, out_ref):
-    parts = t_ref.shape[0]
-    total = t_ref[0].astype(jnp.float32) * dens_ref[0]
-    for p in range(1, parts):
-        total += t_ref[p].astype(jnp.float32) * dens_ref[p]
-    out_ref[...] = (total * mask_ref[0].astype(jnp.float32)).astype(out_ref.dtype)
-
-
-def coulomb_call(densities, fitted, mask_rows):
+def coulomb_kernel(place_ref, dens_ref, ta_ref, ma_ref, tk_ref, mk_ref, away_ref, kept_ref):
+    for t_ref, mask_ref, out_ref in ((ta_ref, ma_ref, away_ref), (tk_ref, mk_ref, kept_ref)):
+        total = t_ref[0].astype(jnp.float32) * dens_ref[0]
+        for p in range(1, t_ref.shape[0]):
+            total += t_ref[p].astype(jnp.float32) * dens_ref[p]
+        out_ref[...] = (total * mask_ref[0].astype(jnp.float32)).astype(out_ref.dtype)
+
+
+def coulomb_call(place, densities, fitted, mask_rows, half):
     parts, rows, cols = fitted.shape
+    tile = min(BLK, half)
+    steps = half // tile
+
+    def away_tile(i, place_ref):
+        return (place_ref[1] * 2 + 1 - place_ref[0]) * steps + i
+
+    def kept_tile(i, place_ref):
+        return (place_ref[1] * 2 + place_ref[0]) * steps + i
+
+    def tensor_spec(which):
+        return pl.BlockSpec((parts, tile, cols), lambda i, place_ref, d: (0, which(i, place_ref), 0))
+
+    def mask_spec(which):
+        return pl.BlockSpec(
+            (1, 1, cols), lambda i, place_ref, d: (which(i, place_ref) * tile // BLK, 0, 0)
+        )
+
     return pl.pallas_call(
         coulomb_kernel,
-        grid=(rows // BLK,),
-        in_specs=[
-            pl.BlockSpec(memory_space=pltpu.SMEM),
-            pl.BlockSpec((parts, BLK, cols), lambda i: (0, i, 0)),
-            pl.BlockSpec((1, 1, cols), lambda i: (i, 0, 0)),
-        ],
-        out_specs=pl.BlockSpec((BLK, cols), lambda i: (i, 0)),
-        out_shape=jax.ShapeDtypeStruct((rows, cols), jnp.bfloat16),
+        grid_spec=pltpu.PrefetchScalarGridSpec(
+            num_scalar_prefetch=2,
+            grid=(steps,),
+            in_specs=[
+                tensor_spec(away_tile),
+                mask_spec(away_tile),
+                tensor_spec(kept_tile),
+                mask_spec(kept_tile),
+            ],
+            out_specs=[pl.BlockSpec((tile, cols), lambda i, place_ref, d: (i, 0))] * 2,
+        ),
+        out_shape=[jax.ShapeDtypeStruct((half, cols), jnp.bfloat16)] * 2,
         compiler_params=pltpu.CompilerParams(vmem_limit_bytes=VMEM_LIMIT),
         cost_estimate=pl.CostEstimate(
-            flops=2 * parts * rows * cols,
-            bytes_accessed=2 * rows * cols * (parts + 1),
+            flops=4 * parts * half * cols,
+            bytes_accessed=4 * half * cols * (parts + 1),
             transcendentals=0,
         ),
         name="coulomb",
-    )(densities, fitted, mask_rows)
-
-
-def fock_kernel(place_ref, own_ref, all_ref, coul_ref, field_ref, out_ref):
+    )(place, densities, fitted, mask_rows, fitted, mask_rows)
+
+
+def fock_kernel(shifts, place_ref, own_ref, mate_ref, all_ref, mate_all_ref, field_ref, *refs):
+    mine, theirs, out_ref = refs[:shifts], refs[shifts : 2 * shifts], refs[2 * shifts]
     parts = own_ref.shape[0]
     rows, cols = out_ref.shape
     half = rows // 2
+    per_src = mine[0].shape[1] // cols
     dims = (((1,), (1,)), ((), ()))
-    total = lax.dot_general(own_ref[0], all_ref[0], dims, preferred_element_type=jnp.float32)
-    for p in range(1, parts):
-        total += lax.dot_general(own_ref[p], all_ref[p], dims, preferred_element_type=jnp.float32)
-    out_ref[...] = -0.5 * total
-    first_row = pl.multiple_of(place_ref[0] * half, half)
-    out_ref[pl.ds(first_row, half), :] += coul_ref[0].astype(jnp.float32)
-
-    col0 = pl.program_id(0) * cols
-    row0 = place_ref[1]
-
-    @pl.when((place_ref[0] == 0) & (row0 < col0 + cols) & (row0 + rows > col0))
+    grp_id, row0, orb_id = place_ref[0], place_ref[1], place_ref[2]
+
+    def slab(a, b):
+        total = lax.dot_general(a[0], b[0], dims, preferred_element_type=jnp.float32)
+        for p in range(1, parts):
+            total += lax.dot_general(a[p], b[p], dims, preferred_element_type=jnp.float32)
+        return total
+
+    out_ref[...] = -0.5 * (slab(own_ref, all_ref) + slab(mate_ref, mate_all_ref))
+
+    step = pl.program_id(0)
+    shift = lax.rem(orb_id - step // per_src + shifts, shifts)
+    col_in = pl.multiple_of(lax.rem(step, per_src) * cols, cols)
+    own_row = pl.multiple_of(grp_id * half, half)
+    mate_row = pl.multiple_of((1 - grp_id) * half, half)
+    for k in range(shifts):
+
+        @pl.when(shift == k)
+        def _():
+            out_ref[pl.ds(own_row, half), :] += mine[k][:, pl.ds(col_in, cols)].astype(jnp.float32)
+            out_ref[pl.ds(mate_row, half), :] += theirs[k][:, pl.ds(col_in, cols)].astype(jnp.float32)
+
+    col0 = step * cols
+
+    @pl.when((row0 < col0 + cols) & (row0 + rows > col0))
     def _():
         row_ids = row0 + lax.broadcasted_iota(jnp.int32, (rows, cols), 0)
         col_ids = col0 + lax.broadcasted_iota(jnp.int32, (rows, cols), 1)
         out_ref[...] += jnp.where(row_ids == col_ids, field_ref[...], jnp.float32(0.0))
 
 
-def fock_call(place, x_own, x_all, coul, field_col):
+def fock_call(place, x_own, x_mate, x_all, x_mate_all, field_col, mine, theirs):
     parts, rows, nocc = x_own.shape
     total = x_all.shape[1]
-    per_src = coul.shape[2]
+    half, per_src = mine[0].shape
     cols = min(1024, per_src)
-    step = per_src // cols
+    own_spec = pl.BlockSpec((parts, rows, nocc), lambda j: (0, 0, 0))
+    all_spec = pl.BlockSpec((parts, cols, nocc), lambda j: (0, j, 0))
     return pl.pallas_call(
-        fock_kernel,
+        functools.partial(fock_kernel, len(mine)),
         grid=(total // cols,),
         in_specs=[
             pl.BlockSpec(memory_space=pltpu.SMEM),
-            pl.BlockSpec((parts, rows, nocc), lambda j: (0, 0, 0)),
-            pl.BlockSpec((parts, cols, nocc), lambda j: (0, j, 0)),
-            pl.BlockSpec((1, rows // 2, cols), lambda j: (j // step, 0, j % step)),
+            own_spec,
+            own_spec,
+            all_spec,
+            all_spec,
             pl.BlockSpec((rows, 1), lambda j: (0, 0)),
-        ],
+        ]
+        + [pl.BlockSpec((half, per_src), lambda j: (0, 0))] * (2 * len(mine)),
         out_specs=pl.BlockSpec((rows, cols), lambda j: (0, j)),
         out_shape=jax.ShapeDtypeStruct((rows, total), jnp.float32),
         compiler_params=pltpu.CompilerParams(vmem_limit_bytes=VMEM_LIMIT),
         cost_estimate=pl.CostEstimate(
-            flops=2 * parts * rows * total * nocc,
-            bytes_accessed=2 * parts * total * nocc + 4 * rows * total + rows * total,
+            flops=4 * parts * rows * total * nocc,
+            bytes_accessed=4 * parts * total * nocc + 4 * rows * total + 2 * rows * total,
             transcendentals=0,
         ),
         name="fock",
-    )(place, x_own, x_all, coul, field_col)
+    )(place, x_own, x_mate, x_all, x_mate_all, field_col, *mine, *theirs)
+
+
+def swap(value):
+    return lax.ppermute(value, "grp", [(0, 1), (1, 0)])
 
 
 def per_device(
@@ -154,6 +198,7 @@
     nocc = orbitals.shape[1]
     orb_count = lax.axis_size("orb")
     aux_count = lax.axis_size("aux")
+    grp_count = lax.axis_size("grp")
     grp_id = lax.axis_index("grp")
     aux_id = lax.axis_index("aux")
     orb_id = lax.axis_index("orb")
@@ -169,7 +214,12 @@
             for a in range(aux_count)
             for o in range(orb_count)
         ]
-        window_c = lax.ppermute(orbitals, ("aux", "orb"), perm)
+        c_half = lax.dynamic_slice_in_dim(orbitals, grp_id * (row_span // 2), row_span // 2, 0)
+        c_half = lax.ppermute(c_half, ("aux", "orb"), perm)
+        c_mate = swap(c_half)
+        window_c = jnp.where(
+            grp_id == 0, jnp.stack([c_half, c_mate]), jnp.stack([c_mate, c_half])
+        ).reshape(col_span, nocc)
     else:
         whole_c = lax.all_gather(orbitals, "aux", axis=0, tiled=True)
         window_c = lax.dynamic_slice_in_dim(whole_c, col_start, col_span, 0)
@@ -180,24 +230,6 @@
         (row_span // BLK, col_span // BLK),
     ).astype(jnp.bfloat16)
     mask_rows = jnp.repeat(bits, BLK, axis=1)[:, None, :]
-
-    x_part, dens_lanes = products_call(fitted_tensor, mask_rows, window_c, orbitals)
-    dens_part = 2.0 * jnp.sum(dens_lanes, axis=(1, 2))
-    densities = lax.psum(dens_part, ("aux", "orb")).astype(jnp.bfloat16).astype(jnp.float32)
-
-    x_swap = lax.all_to_all(
-        x_part.reshape(parts, orb_count, own_span, nocc), "orb", split_axis=1, concat_axis=1, tiled=True
-    )
-    x_own = jnp.sum(x_swap.astype(jnp.float32), axis=1).astype(jnp.bfloat16)
-    x_all = lax.all_gather(x_own, ("aux", "orb"), axis=1, tiled=True)
-
-    coul = coulomb_call(densities, fitted_tensor, mask_rows)
-    coul = coul.reshape(orb_count, 2, half, col_span)
-    away = lax.dynamic_index_in_dim(coul, 1 - grp_id, 1, keepdims=False)
-    kept = lax.dynamic_index_in_dim(coul, grp_id, 1, keepdims=False)
-    got = lax.ppermute(away, "grp", [(0, 1), (1, 0)])
-    both = (kept.astype(jnp.float32) + got.astype(jnp.float32)).astype(jnp.bfloat16)
-    coul_rows = lax.all_to_all(both, "orb", split_axis=0, concat_axis=0, tiled=True)
 
     own_float = orbitals.astype(jnp.float32)
     own_population = 2.0 * jnp.sum(own_float * own_float, axis=1)
@@ -214,13 +246,40 @@
         picker.shape[0], BLK
     )
     field_part = jnp.dot(picker.T, contrib, precision=lax.Precision.HIGHEST)
-    field_vec = lax.psum(field_part, ("grp", "aux", "orb")).reshape(-1)
+
+    x_part, dens_lanes = products_call(fitted_tensor, mask_rows, window_c, orbitals)
+    dens_part = 2.0 * jnp.sum(dens_lanes, axis=(1, 2))
+    dens_slots = jnp.zeros((grp_count, BLK), jnp.float32)
+    dens_slots = lax.dynamic_update_slice(dens_slots, dens_part[None, :], (grp_id, 0))
+    sums = lax.psum(jnp.concatenate([field_part, dens_slots], axis=0), ("grp", "aux", "orb"))
+    field_vec = sums[:block_total].reshape(-1)
+    densities = lax.dynamic_slice(sums, (block_total + grp_id, 0), (1, parts))[0]
+
+    x_blocks = x_part.reshape(parts, orb_count, own_span, nocc)
+    x_sum = lax.dynamic_index_in_dim(x_blocks, orb_id, 1, keepdims=False).astype(jnp.float32)
+    mine, theirs = [], []
+    targets = [lax.rem(orb_id + k, orb_count) for k in range(orb_count)]
+    moves = [[(s, (s + k) % orb_count) for s in range(orb_count)] for k in range(orb_count)]
+    for k in range(1, orb_count):
+        block = lax.dynamic_index_in_dim(x_blocks, targets[k], 1, keepdims=False)
+        x_sum += lax.ppermute(block, "orb", moves[k]).astype(jnp.float32)
+    x_own = x_sum.astype(jnp.bfloat16)
+    x_mate = swap(x_own)
+    x_all = lax.all_gather(x_own, ("aux", "orb"), axis=1, tiled=True)
+    x_mate_all = swap(x_all)
+
+    mine, theirs = [None] * orb_count, [None] * orb_count
+    for k in list(range(1, orb_count)) + [0]:
+        at = jnp.stack([grp_id, targets[k]]).astype(jnp.int32)
+        away, kept = coulomb_call(at, densities, fitted_tensor, mask_rows, half)
+        both = (kept.astype(jnp.float32) + swap(away).astype(jnp.float32)).astype(jnp.bfloat16)
+        mine[k] = lax.ppermute(both, "orb", moves[k]) if k else both
+        theirs[k] = swap(mine[k])
 
     own_first = row_start + orb_id * own_span
     field_col = lax.dynamic_slice_in_dim(field_vec, own_first, own_span, 0)[:, None]
-    place = jnp.stack([grp_id, own_first]).astype(jnp.int32)
-    fock_part = fock_call(place, x_own, x_all, coul_rows, field_col)
-    fock = lax.psum(fock_part, "grp")
+    place = jnp.stack([grp_id, own_first, orb_id]).astype(jnp.int32)
+    fock = fock_call(place, x_own, x_mate, x_all, x_mate_all, field_col, mine, theirs)
     return (fock, mm_potential)
 
 

time: 465 us -> 427 us (0.918)
  blocking collectives: 309 us -> 51.3 us
  waiting for transfers between devices: 55.5 us -> 247 us
  starting transfers between devices: 7.05 us -> 47.4 us
  local copies, waits for them, and re-layouts: 19.4 us -> 3.9 us
    psum x2 -> x1, blocking collectives: 180 us -> 42.2 us  [per_device(): lax.psum(jnp.concatenate([field_part, dens_slots], axis=0), ('grp', 'aux'...]
    all_gather x1, waiting for transfers between devices: 0.01 us -> 124 us  [per_device(): x_all = lax.all_gather(x_own, ('aux', 'orb'), axis=1, tiled=True)]
    all_to_all x1 -> x0, blocking collectives: 120 us -> none  [per_device(): lax.all_to_all(x_part.reshape(parts, orb_count, own_span, nocc), 'orb', s...]
    ppermute x2 -> x18, waiting for transfers between devices: 7.5 us -> 123 us  [the longest x3 85.7 us: per_device(): mine[k] = lax.ppermute(both, 'orb', moves[k]) if k else both]
    psum x1 -> x0, waiting for transfers between devices: 48 us -> none  [per_device(): fock = lax.psum(fock_part, 'grp')]
    ppermute x2 -> x18, starting transfers between devices: 1.89 us -> 47.3 us  [the longest x3 40.6 us: per_device(): x_sum += lax.ppermute(block, 'orb', moves[k]).astype(jnp.float32)]
    unnamed x20 -> x19, local copies, waits for them, and re-layouts: 14.1 us -> 1.04 us
    all_to_all x1 -> x0, starting transfers between devices: 5.08 us -> none  [per_device(): lax.all_to_all(both, 'orb', split_axis=0, concat_axis=0, tiled=True)]
  transfers between devices with their start and end apart: 5 -> 19, of which waited for: 2 -> 8; matrix products, arithmetic and copies ran while one was open for 4% -> 2% of each run, Pallas kernels for 3% -> 3%
where the time goes in v2:
time: 427 us; the launch traced here: 426 us
  waiting for transfers between devices  247 us (58%)
  blocking collectives  51.3 us (12%)
  Pallas kernels  49.4 us (12%)
  starting transfers between devices  47.4 us (11%)
  between operations  14.4 us (3%)
  other arithmetic  8.5 us (2%)
    all_gather x1, waiting for transfers between devices, per_device(): x_all = lax.all_gather(x_own, ('aux', 'orb'), axis=1, tiled=True)  124 us
    ppermute x3, waiting for transfers between devices, per_device(): mine[k] = lax.ppermute(both, 'orb', moves[k]) if k else both  85.7 us
    psum x1, blocking collectives, per_device(): lax.psum(jnp.concatenate([field_part, dens_slots], axis=0), ('grp', 'aux'...  42.2 us
    ppermute x3, starting transfers between devices, per_device(): x_sum += lax.ppermute(block, 'orb', moves[k]).astype(jnp.float32)  40.6 us
    ppermute x3, waiting for transfers between devices, per_device(): x_sum += lax.ppermute(block, 'orb', moves[k]).astype(jnp.float32)  34.7 us
    pallas_call x1, Pallas kernels, fock_call(): pl.pallas_call(functools.partial(fock_kernel, len(mine)), grid=(total //...  20.7 us
    pallas_call x1, Pallas kernels, products_call(): pl.pallas_call(products_kernel, grid=(rows // BLK,), in_specs=[pl.BlockSp...  14.7 us
    pallas_call x4, Pallas kernels, coulomb_call(): pl.pallas_call(coulomb_kernel, grid_spec=pltpu.PrefetchScalarGridSpec(num...  14 us
  transfers between devices with their start and end apart: 19, of which 8 were waited for; matrix products, arithmetic and copies ran while one was open for 2% of the time, Pallas kernels for 3%

profile of v2, /device:TPU:0, one launch (start us, length us, event | category | flops | bytes accessed | tf_op | source)
XLA Modules:
  0.0 425.9 jit_solution(9311057379279235900)
XLA Ops:
  7.2 0.0 copy-start
  7.2 0.0 all-gather.2.cloned.1.call-start
  7.2 1.2 constant_dynamic-slice_fusion.1
  8.4 0.7 collective-permute-start
  9.1 0.0 collective-permute-done
  9.1 0.5 collective-permute-start.1
  9.6 0.8 fusion.12
  10.4 0.1 broadcast_in_dim.12
  10.6 0.6 collective-permute-done.1
  11.2 0.2 maximum_select_fusion
  11.4 14.7 %products.1 = (bf16[2,2048,256]{2,1,0:T(8,128)(2,1)S(1)}, f32[2,8,256]{2,1,0:T(8,128)S(1)}) custom-call(bf16[2,2048,2048]{2,1,0:T(8,128)(2,1)} %tk_ref.7, bf16[16,1,2048]{2,1,0:T(2,128)(2,1)S(1)} %broadcast_in_dim_reshape.5.mask_ref.ma_ref.mk_ref, bf16[2048,256]{1,0:T(8,128)(2,1)S(1)} %bitcast.60, bf16[2048,256]{1,0:T(8,128)(2,1)S(1)} %copy-done.2), custom_call_target="tpu_custom_call" | custom-call | flops 4294967296 | bytes 18874368 | tf_op jit(solution)/shard_map/products/pallas_call | solution.py:43
  26.1 1.2 dynamic-slice_bitcast_fusion.2
  27.3 39.1 %collective-permute-start.2 = (bf16[2,512,256]{2,1,0:T(8,128)(2,1)}, bf16[2,512,256]{2,1,0:T(8,128)(2,1)}, u32[]{:S(2)}, u32[]{:S(2)}) collective-permute-start(bf16[2,512,256]{2,1,0:T(8,128)(2,1)} %get-tuple-element.22), channel_id=1, source_target_pairs={{0,1},{1,2},{2,3},{3,0},{4,5},{5,6},{6,7},{7,4},{8,9},{9,10},{10,1... | collective-permute-start | bytes 1572872 | tf_op jit(solution)/shard_map/ppermute | solution.py:265
  66.4 0.0 collective-permute-start.4
  66.4 1.5 collective-permute-start.3
  67.9 11.1 %collective-permute-done.2 = bf16[2,512,256]{2,1,0:T(8,128)(2,1)} collective-permute-done((bf16[2,512,256]{2,1,0:T(8,128)(2,1)}, bf16[2,512,256]{2,1,0:T(8,128)(2,1)}, u32[]{:S(2)}, u32[]{:S(2)}) %collective-permute-start.2) | collective-permute-done | bytes 524320 | tf_op jit(solution)/shard_map/ppermute | solution.py:265
  79.0 11.3 %collective-permute-done.4 = bf16[2,512,256]{2,1,0:T(8,128)(2,1)} collective-permute-done((bf16[2,512,256]{2,1,0:T(8,128)(2,1)}, bf16[2,512,256]{2,1,0:T(8,128)(2,1)}, u32[]{:S(2)}, u32[]{:S(2)}) %collective-permute-start.4) | collective-permute-done | bytes 524320 | tf_op jit(solution)/shard_map/ppermute | solution.py:265
  90.2 12.3 %collective-permute-done.3 = bf16[2,512,256]{2,1,0:T(8,128)(2,1)} collective-permute-done((bf16[2,512,256]{2,1,0:T(8,128)(2,1)}, bf16[2,512,256]{2,1,0:T(8,128)(2,1)}, u32[]{:S(2)}, u32[]{:S(2)}) %collective-permute-start.3) | collective-permute-done | bytes 524320 | tf_op jit(solution)/shard_map/ppermute | solution.py:265
  102.6 2.4 fusion.2.own_ref
  105.0 0.0 all-gather.2.cloned.1.call-update
  105.0 124.4 %all-gather.2.cloned.1.call-done.all_ref = bf16[2,8192,256]{2,1,0:T(8,128)(2,1)} async-done(((bf16[2,512,256]{2,1,0:T(8,128)(2,1)}), bf16[2,8192,256]{2,1,0:T(8,128)(2,1)}) %all-gather.2.cloned.1.call-update) | async-done | bytes 8388624 | tf_op jit(solution)/shard_map/all_gather | solution.py:268
  229.4 0.0 collective-permute-start.6
  229.4 0.2 convolution_bitcast_fusion
  229.6 0.1 pad_add_fusion.4.place_ref
  229.7 0.4 multiply_reduce_fusion
  230.1 1.0 copy-done.4
  231.1 1.0 fusion.4
  232.0 0.3 fusion.14
  232.3 0.1 reduce_sum.28
  232.4 0.2 dynamic_update_slice.3
  232.6 42.2 %psum.7 = f32[66,128]{1,0:T(8,128)S(1)} all-reduce(f32[66,128]{1,0:T(8,128)S(1)} %pad_maximum_fusion), channel_id=1, replica_groups=mesh['grp'=2,'aux'=4,'orb'=4] {'grp','aux','orb'}, use_global_device_ids=true, to_apply=%region_2.3 | all-reduce | flops 8448 | bytes 67584 | tf_op jit(solution)/shard_map/psum | solution.py:254
  274.9 3.8 coulomb.7
  278.6 0.1 pad_add_fusion.2
  278.7 3.8 coulomb.6
  282.5 0.5 collective-permute-start.10
  283.0 0.1 pad_add_fusion.1.place_ref
  283.1 3.2 coulomb.5
  286.3 0.1 collective-permute-start.8
  286.4 3.2 coulomb.4
  289.6 0.6 collective-permute-start.7
  290.2 0.0 collective-permute-done.12
  290.2 1.6 add_convert_fusion
  291.8 2.3 collective-permute-start.13
  294.2 0.0 collective-permute-done.10
  294.2 1.6 add_convert_fusion.1
  295.8 0.7 collective-permute-start.11
  296.5 0.4 add_convert_fusion.2
  296.9 0.7 collective-permute-start.9
  297.6 0.0 copy-start.6
  297.6 0.4 add_convert_fusion.3.refs_0_
  298.0 1.5 collective-permute-done.5.mate_ref
  299.5 0.1 collective-permute-start.14
  299.6 18.2 %collective-permute-done.13.refs_3_ = bf16[256,2048]{1,0:T(8,128)(2,1)} collective-permute-done((bf16[256,2048]{1,0:T(8,128)(2,1)S(1)}, bf16[256,2048]{1,0:T(8,128)(2,1)}, u32[]{:S(2)}, u32[]{:S(2)}) %collective-permute-start.13) | collective-permute-done | bytes 1048608 | tf_op jit(solution)/shard_map/ppermute | solution.py:276
  317.8 67.6 %collective-permute-done.11.refs_2_ = bf16[256,2048]{1,0:T(8,128)(2,1)} collective-permute-done((bf16[256,2048]{1,0:T(8,128)(2,1)S(1)}, bf16[256,2048]{1,0:T(8,128)(2,1)}, u32[]{:S(2)}, u32[]{:S(2)}) %collective-permute-start.11) | collective-permute-done | bytes 1048608 | tf_op jit(solution)/shard_map/ppermute | solution.py:276
  385.3 0.5 collective-permute-start.15
  385.9 0.3 multiply_reduce_fusion.1
  386.2 9.1 %all_gather.7 = f32[8192]{0:T(1024)S(1)} all-gather(f32[2048]{0:T(1024)S(1)} %broadcast_multiply_fusion), channel_id=1, replica_groups=mesh['grp'=2,'aux'=4,'orb'=4] {'aux'}, dimensions={0}, use_global_device_ids=true | all-gather | bytes 40960 | tf_op jit(solution)/shard_map/all_gather | solution.py:236
  395.3 0.1 pad_add_fusion.place_ref
  395.4 0.2 fusion.9
  395.6 2.5 fusion.3
  398.1 0.1 dynamic_slice.31
  398.2 0.1 copy.42.field_ref
  398.4 0.0 copy-start.1
  398.4 20.7 %fock.1 = f32[512,8192]{1,0:T(8,128)} custom-call(s32[3]{0:T(128)S(1)} %pad_add_fusion.place_ref, bf16[2,512,256]{2,1,0:T(8,128)(2,1)S(1)} %copy-done.3, bf16[2,512,256]{2,1,0:T(8,128)(2,1)S(1)} %collective-permute-done.5.mate_ref, bf16[2,8192,256]{2,1,0:T(8,128)(2,1)} %all-gather.2.cloned.1.call-done.all_ref, ...), custom_call_target="tpu_custom_call" | custom-call | flops 8589934592 | bytes 41943040 | tf_op jit(solution)/shard_map/fock/pallas_call | solution.py:166
  (34 shorter events, 0.1 us)
Async XLA Ops:
  7.2 222.9 %copy-start = (f32[1024]{0:T(1024)S(1)}, f32[1024]{0:T(1024)}, u32[]{:S(2)}) copy-start(f32[1024]{0:T(1024)} %param.14) | copy-start | bytes 12292
  7.2 4.2 copy-start.2
  7.2 222.2 %all-gather.2.cloned.1.call-start = ((), (), s32[]{:S(2)}) async-start(), calls=%async_computation | async-start | bytes 8912896 | tf_op jit(solution)/shard_map/all_gather | solution.py:268
  8.4 0.7 collective-permute-start
  9.1 2.1 collective-permute-start.1
  27.3 202.1 %copy-start.5 = (f32[3,8192]{1,0:T(4,128)S(1)}, f32[3,8192]{1,0:T(4,128)}, u32[]{:S(2)}) copy-start(f32[3,8192]{1,0:T(4,128)} %param.12) | copy-start | bytes 294916
  27.3 202.1 %copy-start.8 = (s32[1,2]{1,0:T(1,128)S(1)}, s32[1,2]{1,0:T(1,128)}, u32[]{:S(2)}) copy-start(s32[1,2]{1,0:T(1,128)} %param.15) | copy-start | bytes 28
  27.3 202.4 %copy-start.7 = (f32[3,1024]{1,0:T(4,128)S(1)}, f32[3,1024]{1,0:T(4,128)}, u32[]{:S(2)}) copy-start(f32[3,1024]{1,0:T(4,128)} %param.13) | copy-start | bytes 36868
  27.3 51.7 %collective-permute-start.2 = (bf16[2,512,256]{2,1,0:T(8,128)(2,1)}, bf16[2,512,256]{2,1,0:T(8,128)(2,1)}, u32[]{:S(2)}, u32[]{:S(2)}) collective-permute-start(bf16[2,512,256]{2,1,0:T(8,128)(2,1)} %get-tuple-element.22), channel_id=1, source_target_pairs={{0,1},{1,2},{2,3},{3,0},{4,5},{5,6},{6,7},{7,4},{8,9},{9,10},{10,1... | collective-permute-start | bytes 1572872 | tf_op jit(solution)/shard_map/ppermute | solution.py:265
  66.4 23.9 %collective-permute-start.4 = (bf16[2,512,256]{2,1,0:T(8,128)(2,1)}, bf16[2,512,256]{2,1,0:T(8,128)(2,1)}, u32[]{:S(2)}, u32[]{:S(2)}) collective-permute-start(bf16[2,512,256]{2,1,0:T(8,128)(2,1)} %get-tuple-element.23), channel_id=1, source_target_pairs={{0,3},{1,0},{2,1},{3,2},{4,7},{5,4},{6,5},{7,6},{8,11},{9,8},{10,9... | collective-permute-start | bytes 1572872 | tf_op jit(solution)/shard_map/ppermute | solution.py:265
  66.4 36.2 %collective-permute-start.3 = (bf16[2,512,256]{2,1,0:T(8,128)(2,1)}, bf16[2,512,256]{2,1,0:T(8,128)(2,1)}, u32[]{:S(2)}, u32[]{:S(2)}) collective-permute-start(bf16[2,512,256]{2,1,0:T(8,128)(2,1)} %get-tuple-element.24), channel_id=1, source_target_pairs={{0,2},{1,3},{2,0},{3,1},{4,6},{5,7},{6,4},{7,5},{8,10},{9,11},{10,... | collective-permute-start | bytes 1572872 | tf_op jit(solution)/shard_map/ppermute | solution.py:265
  229.4 169.0 %collective-permute-start.6 = (bf16[2,8192,256]{2,1,0:T(8,128)(2,1)}, bf16[2,8192,256]{2,1,0:T(8,128)(2,1)}, u32[]{:S(2)}, u32[]{:S(2)}) collective-permute-start(bf16[2,8192,256]{2,1,0:T(8,128)(2,1)} %all-gather.2.cloned.1.call-done.all_ref), channel_id=1, source_target_pairs={{0,16},{16,0},{1,17},{17,1},{2,18},{18,2},{3,19},{19,3},{4,20},{20... | collective-permute-start | bytes 25165832 | tf_op jit(solution)/shard_map/ppermute | solution.py:191
  230.1 1.0 copy-start.4
  278.6 11.6 %collective-permute-start.12 = (bf16[256,2048]{1,0:T(8,128)(2,1)}, bf16[256,2048]{1,0:T(8,128)(2,1)}, u32[]{:S(2)}, u32[]{:S(2)}) collective-permute-start(bf16[256,2048]{1,0:T(8,128)(2,1)} %get-tuple-element.21), channel_id=1, source_target_pairs={{0,16},{16,0},{1,17},{17,1},{2,18},{18,2},{3,19},{19,3},{4,20},{20... | collective-permute-start | bytes 3145736 | tf_op jit(solution)/shard_map/ppermute | solution.py:191
  282.5 11.7 %collective-permute-start.10 = (bf16[256,2048]{1,0:T(8,128)(2,1)}, bf16[256,2048]{1,0:T(8,128)(2,1)}, u32[]{:S(2)}, u32[]{:S(2)}) collective-permute-start(bf16[256,2048]{1,0:T(8,128)(2,1)} %get-tuple-element.19), channel_id=1, source_target_pairs={{0,16},{16,0},{1,17},{17,1},{2,18},{18,2},{3,19},{19,3},{4,20},{20... | collective-permute-start | bytes 3145736 | tf_op jit(solution)/shard_map/ppermute | solution.py:191
  286.3 10.1 %collective-permute-start.8 = (bf16[256,2048]{1,0:T(8,128)(2,1)S(1)}, bf16[256,2048]{1,0:T(8,128)(2,1)S(1)}, u32[]{:S(2)}, u32[]{:S(2)}) collective-permute-start(bf16[256,2048]{1,0:T(8,128)(2,1)S(1)} %get-tuple-element.17), channel_id=1, source_target_pairs={{0,16},{16,0},{1,17},{17,1},{2,18},{18,2},{3,19},{19,3},{4,20},{20... | collective-permute-start | bytes 3145736 | tf_op jit(solution)/shard_map/ppermute | solution.py:191
  289.6 7.9 %collective-permute-start.7 = (bf16[256,2048]{1,0:T(8,128)(2,1)S(1)}, bf16[256,2048]{1,0:T(8,128)(2,1)S(1)}, u32[]{:S(2)}, u32[]{:S(2)}) collective-permute-start(bf16[256,2048]{1,0:T(8,128)(2,1)S(1)} %get-tuple-element.15), channel_id=1, source_target_pairs={{0,16},{16,0},{1,17},{17,1},{2,18},{18,2},{3,19},{19,3},{4,20},{20... | collective-permute-start | bytes 3145736 | tf_op jit(solution)/shard_map/ppermute | solution.py:191
  291.8 26.0 %collective-permute-start.13 = (bf16[256,2048]{1,0:T(8,128)(2,1)S(1)}, bf16[256,2048]{1,0:T(8,128)(2,1)}, u32[]{:S(2)}, u32[]{:S(2)}) collective-permute-start(bf16[256,2048]{1,0:T(8,128)(2,1)S(1)} %add_convert_fusion), channel_id=1, source_target_pairs={{0,3},{1,0},{2,1},{3,2},{4,7},{5,4},{6,5},{7,6},{8,11},{9,8},{10,9... | collective-permute-start | bytes 3145736 | tf_op jit(solution)/shard_map/ppermute | solution.py:276
  295.8 1.8 copy-start.3
  295.8 89.5 %collective-permute-start.11 = (bf16[256,2048]{1,0:T(8,128)(2,1)S(1)}, bf16[256,2048]{1,0:T(8,128)(2,1)}, u32[]{:S(2)}, u32[]{:S(2)}) collective-permute-start(bf16[256,2048]{1,0:T(8,128)(2,1)S(1)} %add_convert_fusion.1), channel_id=1, source_target_pairs={{0,2},{1,3},{2,0},{3,1},{4,6},{5,7},{6,4},{7,5},{8,10},{9,11},{10,... | collective-permute-start | bytes 3145736 | tf_op jit(solution)/shard_map/ppermute | solution.py:276
  296.9 88.5 %collective-permute-start.9 = (bf16[256,2048]{1,0:T(8,128)(2,1)S(1)}, bf16[256,2048]{1,0:T(8,128)(2,1)}, u32[]{:S(2)}, u32[]{:S(2)}) collective-permute-start(bf16[256,2048]{1,0:T(8,128)(2,1)S(1)} %add_convert_fusion.2), channel_id=1, source_target_pairs={{0,1},{1,2},{2,3},{3,0},{4,5},{5,6},{6,7},{7,4},{8,9},{9,10},{10,1... | collective-permute-start | bytes 3145736 | tf_op jit(solution)/shard_map/ppermute | solution.py:276
  297.6 1.9 collective-permute-start.5
  297.6 97.8 %copy-start.6 = (f32[8192]{0:T(1024)S(1)}, f32[8192]{0:T(1024)}, u32[]{:S(2)}) copy-start(f32[8192]{0:T(1024)} %param.11) | copy-start | bytes 98308
  299.5 98.8 %collective-permute-start.14 = (bf16[256,2048]{1,0:T(8,128)(2,1)S(1)}, bf16[256,2048]{1,0:T(8,128)(2,1)}, u32[]{:S(2)}, u32[]{:S(2)}) collective-permute-start(bf16[256,2048]{1,0:T(8,128)(2,1)S(1)} %add_convert_fusion.3.refs_0_), channel_id=1, source_target_pairs={{0,16},{16,0},{1,17},{17,1},{2,18},{18,2},{3,19},{19,3},{4,20},{20... | collective-permute-start | bytes 3145736 | tf_op jit(solution)/shard_map/ppermute | solution.py:191
  317.8 80.6 %collective-permute-start.17 = (bf16[256,2048]{1,0:T(8,128)(2,1)}, bf16[256,2048]{1,0:T(8,128)(2,1)}, u32[]{:S(2)}, u32[]{:S(2)}) collective-permute-start(bf16[256,2048]{1,0:T(8,128)(2,1)} %collective-permute-done.13.refs_3_), channel_id=1, source_target_pairs={{0,16},{16,0},{1,17},{17,1},{2,18},{18,2},{3,19},{19,3},{4,20},{20... | collective-permute-start | bytes 3145736 | tf_op jit(solution)/shard_map/ppermute | solution.py:191
  385.3 13.0 %collective-permute-start.16 = (bf16[256,2048]{1,0:T(8,128)(2,1)}, bf16[256,2048]{1,0:T(8,128)(2,1)}, u32[]{:S(2)}, u32[]{:S(2)}) collective-permute-start(bf16[256,2048]{1,0:T(8,128)(2,1)} %collective-permute-done.11.refs_2_), channel_id=1, source_target_pairs={{0,16},{16,0},{1,17},{17,1},{2,18},{18,2},{3,19},{19,3},{4,20},{20... | collective-permute-start | bytes 3145736 | tf_op jit(solution)/shard_map/ppermute | solution.py:191
  385.3 13.0 %collective-permute-start.15 = (bf16[256,2048]{1,0:T(8,128)(2,1)}, bf16[256,2048]{1,0:T(8,128)(2,1)}, u32[]{:S(2)}, u32[]{:S(2)}) collective-permute-start(bf16[256,2048]{1,0:T(8,128)(2,1)} %collective-permute-done.9.refs_1_), channel_id=1, source_target_pairs={{0,16},{16,0},{1,17},{17,1},{2,18},{18,2},{3,19},{19,3},{4,20},{20... | collective-permute-start | bytes 3145736 | tf_op jit(solution)/shard_map/ppermute | solution.py:191
  398.4 20.7 %copy-start.1 = (f32[1024]{0:T(1024)S(1)}, f32[1024]{0:T(1024)}, u32[]{:S(2)}) copy-start(f32[1024]{0:T(1024)} %param.14) | copy-start | bytes 12292
Sparse Core Ops, SparseCore 0:
  105.1 124.2 all-gather.1

commit v3 on v2

--- a/solution.py
+++ b/solution.py
@@ -13,13 +13,11 @@
 softening = 1.0
 
 
-def near_kernel(picker, centre_blocks, charge_blocks, atom_xyz):
+def near_kernel(picker, centre_blocks, atom_xyz):
     near_xyz = jnp.einsum("kb,cbj->ckj", picker, centre_blocks, precision=lax.Precision.HIGHEST)
     near_xyz = near_xyz.reshape(3, picker.shape[0] * centre_blocks.shape[2])
-    near_q = jnp.dot(picker, charge_blocks, precision=lax.Precision.HIGHEST).reshape(-1)
     offsets = near_xyz[:, :, None] - atom_xyz[:, None, :]
-    kernel = lax.rsqrt(jnp.sum(offsets * offsets, axis=0) + softening)
-    return (kernel, near_q)
+    return lax.rsqrt(jnp.sum(offsets * offsets, axis=0) + softening)
 
 
 def products_kernel(t_ref, mask_ref, win_ref, c_ref, x_ref, dens_ref):
@@ -234,47 +232,54 @@
     own_float = orbitals.astype(jnp.float32)
     own_population = 2.0 * jnp.sum(own_float * own_float, axis=1)
     population = lax.all_gather(own_population, "aux", axis=0, tiled=True)
-    qm_charge = nuclear - population
     centre_blocks = centres.reshape(3, block_total, BLK)
-    charge_blocks = qm_charge.reshape(block_total, BLK)
     picker = (neighbours[0][:, None] == jnp.arange(block_total, dtype=jnp.int32)[None, :]).astype(
         jnp.float32
     )
-    kernel, near_q = near_kernel(picker, centre_blocks, charge_blocks, mm_positions)
-    mm_potential = jnp.dot(near_q, kernel, precision=lax.Precision.HIGHEST)
+    kernel = near_kernel(picker, centre_blocks, mm_positions)
     contrib = jnp.dot(kernel, mm_charges, precision=lax.Precision.HIGHEST).reshape(
         picker.shape[0], BLK
     )
     field_part = jnp.dot(picker.T, contrib, precision=lax.Precision.HIGHEST)
+
+    window_c, population = lax.optimization_barrier((window_c, population))
+    qm_charge = nuclear - population
+    charge_blocks = qm_charge.reshape(block_total, BLK)
+    near_q = jnp.dot(picker, charge_blocks, precision=lax.Precision.HIGHEST).reshape(-1)
+    mm_potential = jnp.dot(near_q, kernel, precision=lax.Precision.HIGHEST)
 
     x_part, dens_lanes = products_call(fitted_tensor, mask_rows, window_c, orbitals)
     dens_part = 2.0 * jnp.sum(dens_lanes, axis=(1, 2))
     dens_slots = jnp.zeros((grp_count, BLK), jnp.float32)
     dens_slots = lax.dynamic_update_slice(dens_slots, dens_part[None, :], (grp_id, 0))
     sums = lax.psum(jnp.concatenate([field_part, dens_slots], axis=0), ("grp", "aux", "orb"))
+
+    x_blocks = x_part.reshape(parts, orb_count, own_span, nocc)
+    targets = [lax.rem(orb_id + k, orb_count) for k in range(orb_count)]
+    moves = [[(s, (s + k) % orb_count) for s in range(orb_count)] for k in range(orb_count)]
+    arrived = []
+    for k in range(1, orb_count):
+        block = lax.dynamic_index_in_dim(x_blocks, targets[k], 1, keepdims=False)
+        arrived.append(lax.ppermute(block, "orb", moves[k]))
+    sums, *arrived = lax.optimization_barrier((sums, *arrived))
     field_vec = sums[:block_total].reshape(-1)
     densities = lax.dynamic_slice(sums, (block_total + grp_id, 0), (1, parts))[0]
-
-    x_blocks = x_part.reshape(parts, orb_count, own_span, nocc)
     x_sum = lax.dynamic_index_in_dim(x_blocks, orb_id, 1, keepdims=False).astype(jnp.float32)
-    mine, theirs = [], []
-    targets = [lax.rem(orb_id + k, orb_count) for k in range(orb_count)]
-    moves = [[(s, (s + k) % orb_count) for s in range(orb_count)] for k in range(orb_count)]
-    for k in range(1, orb_count):
-        block = lax.dynamic_index_in_dim(x_blocks, targets[k], 1, keepdims=False)
-        x_sum += lax.ppermute(block, "orb", moves[k]).astype(jnp.float32)
+    for block in arrived:
+        x_sum += block.astype(jnp.float32)
     x_own = x_sum.astype(jnp.bfloat16)
     x_mate = swap(x_own)
     x_all = lax.all_gather(x_own, ("aux", "orb"), axis=1, tiled=True)
-    x_mate_all = swap(x_all)
-
-    mine, theirs = [None] * orb_count, [None] * orb_count
+
+    mine = [None] * orb_count
     for k in list(range(1, orb_count)) + [0]:
         at = jnp.stack([grp_id, targets[k]]).astype(jnp.int32)
         away, kept = coulomb_call(at, densities, fitted_tensor, mask_rows, half)
         both = (kept.astype(jnp.float32) + swap(away).astype(jnp.float32)).astype(jnp.bfloat16)
         mine[k] = lax.ppermute(both, "orb", moves[k]) if k else both
-        theirs[k] = swap(mine[k])
+    x_all, *mine = lax.optimization_barrier((x_all, *mine))
+    theirs = [swap(block) for block in mine]
+    x_mate_all = swap(x_all)
 
     own_first = row_start + orb_id * own_span
     field_col = lax.dynamic_slice_in_dim(field_vec, own_first, own_span, 0)[:, None]

time: 427 us -> 377 us (0.88)
  waiting for transfers between devices: 247 us -> 176 us
  blocking collectives: 51.3 us -> 108 us
  starting transfers between devices: 47.4 us -> 10.9 us
    all_gather x1, waiting for transfers between devices: 124 us -> 34.7 us  [per_device(): x_all = lax.all_gather(x_own, ('aux', 'orb'), axis=1, tiled=True)]
    ppermute x3, waiting for transfers between devices: 85.7 us -> 126 us  [per_device(): mine[k] = lax.ppermute(both, 'orb', moves[k]) if k else both]
    ppermute x3, starting transfers between devices: 40.6 us -> 4.21 us  [per_device(): arrived.append(lax.ppermute(block, 'orb', moves[k]))]
    all_gather x1, blocking collectives: 9.11 us -> 44.5 us  [per_device(): population = lax.all_gather(own_population, 'aux', axis=0, tiled=True)]
    ppermute x3, waiting for transfers between devices: 34.7 us -> 0.01 us  [per_device(): arrived.append(lax.ppermute(block, 'orb', moves[k]))]
    psum x1, blocking collectives: 42.2 us -> 63.9 us  [per_device(): lax.psum(jnp.concatenate([field_part, dens_slots], axis=0), ('grp', 'aux'...]
    ppermute x11, waiting for transfers between devices: 2.11 us -> 15.8 us  [swap(): return lax.ppermute(value, 'grp', [(0, 1), (1, 0)])]
  transfers between devices with their start and end apart: 19 -> 19, of which waited for: 8 -> 6; matrix products, arithmetic and copies ran while one was open for 2% -> 3% of each run, Pallas kernels for 3% -> 4%
where the time goes in v3:
time: 377 us; the launch traced here: 376 us
  waiting for transfers between devices  176 us (47%)
  blocking collectives  108 us (29%)
  Pallas kernels  48.6 us (13%)
  between operations  14.4 us (4%)
  starting transfers between devices  10.9 us (3%)
  other arithmetic  8.52 us (2%)
  matrix products  5.04 us (1%)
    ppermute x3, waiting for transfers between devices, per_device(): mine[k] = lax.ppermute(both, 'orb', moves[k]) if k else both  126 us
    psum x1, blocking collectives, per_device(): lax.psum(jnp.concatenate([field_part, dens_slots], axis=0), ('grp', 'aux'...  63.9 us
    all_gather x1, blocking collectives, per_device(): population = lax.all_gather(own_population, 'aux', axis=0, tiled=True)  44.5 us
    all_gather x1, waiting for transfers between devices, per_device(): x_all = lax.all_gather(x_own, ('aux', 'orb'), axis=1, tiled=True)  34.7 us
    pallas_call x1, Pallas kernels, fock_call(): pl.pallas_call(functools.partial(fock_kernel, len(mine)), grid=(total //...  20.4 us
    ppermute x11, waiting for transfers between devices, swap(): return lax.ppermute(value, 'grp', [(0, 1), (1, 0)])  15.8 us
    pallas_call x1, Pallas kernels, products_call(): pl.pallas_call(products_kernel, grid=(rows // BLK,), in_specs=[pl.BlockSp...  14.7 us
    pallas_call x4, Pallas kernels, coulomb_call(): pl.pallas_call(coulomb_kernel, grid_spec=pltpu.PrefetchScalarGridSpec(num...  13.5 us
  transfers between devices with their start and end apart: 19, of which 6 were waited for; matrix products, arithmetic and copies ran while one was open for 3% of the time, Pallas kernels for 4%

profile of v3, /device:TPU:0, one launch (start us, length us, event | category | flops | bytes accessed | tf_op | source)
XLA Modules:
  0.0 375.9 jit_solution(6270436667691109960)
XLA Ops:
  7.2 0.0 copy-start
  7.2 0.0 all-gather.2.cloned.1.call-start
  7.2 1.1 constant_dynamic-slice_fusion.1
  8.3 0.7 collective-permute-start
  9.1 1.1 convolution_bitcast_fusion
  10.2 1.6 multiply_reduce_fusion.1
  11.8 0.5 collective-permute-start.1
  12.3 0.8 fusion.12
  13.1 0.1 broadcast_in_dim.12
  13.3 44.5 %all_gather.6 = f32[8192]{0:T(1024)S(1)} all-gather(f32[2048]{0:T(1024)S(1)} %broadcast_multiply_fusion), channel_id=1, replica_groups=mesh['grp'=2,'aux'=4,'orb'=4] {'aux'}, dimensions={0}, use_global_device_ids=true | all-gather | bytes 40960 | tf_op jit(solution)/shard_map/all_gather | solution.py:234
  57.8 0.0 copy-start.2
  57.8 0.4 multiply_reduce_fusion
  58.2 1.0 fusion.4
  59.2 0.0 copy-done.6
  59.2 0.2 maximum_select_fusion
  59.4 14.7 %products.1 = (bf16[2,2048,256]{2,1,0:T(8,128)(2,1)S(1)}, f32[2,8,256]{2,1,0:T(8,128)S(1)}) custom-call(bf16[2,2048,2048]{2,1,0:T(8,128)(2,1)} %tk_ref.7, bf16[16,1,2048]{2,1,0:T(2,128)(2,1)S(1)} %broadcast_in_dim_reshape.5.mask_ref.ma_ref.mk_ref, bf16[2048,256]{1,0:T(8,128)(2,1)S(1)} %bitcast.60, bf16[2048,256]{1,0:T(8,128)(2,1)S(1)} %copy-done.2), custom_call_target="tpu_custom_call" | custom-call | flops 4294967296 | bytes 18874368 | tf_op jit(solution)/shard_map/products/pallas_call | solution.py:41
  74.1 0.0 copy-start.9
  74.1 0.9 dynamic-slice_bitcast_fusion
  75.0 3.6 collective-permute-start.4
  78.7 0.6 collective-permute-start.2
  79.2 0.3 fusion.14
  79.5 0.1 reduce_sum.29
  79.6 0.2 dynamic_update_slice.3
  79.8 63.9 %psum.7 = f32[66,128]{1,0:T(8,128)S(1)} all-reduce(f32[66,128]{1,0:T(8,128)S(1)} %pad_maximum_fusion), channel_id=1, replica_groups=mesh['grp'=2,'aux'=4,'orb'=4] {'grp','aux','orb'}, use_global_device_ids=true, to_apply=%region_3.4 | all-reduce | flops 8448 | bytes 67584 | tf_op jit(solution)/shard_map/psum | solution.py:255
  143.8 2.4 fusion.2.own_ref
  146.2 0.0 all-gather.2.cloned.1.call-update
  146.2 0.1 pad_add_fusion.4.place_ref
  146.3 3.2 coulomb.7
  149.5 0.1 collective-permute-start.11
  149.6 0.1 pad_add_fusion.2
  149.7 3.8 %coulomb.6 = (bf16[256,2048]{1,0:T(8,128)(2,1)}, bf16[256,2048]{1,0:T(8,128)(2,1)S(1)}) custom-call(s32[2]{0:T(128)S(1)} %get-tuple-element.48.place_ref, f32[2]{0:T(128)S(1)} %fusion.15.dens_ref, bf16[2,2048,2048]{2,1,0:T(8,128)(2,1)} %tk_ref.7, bf16[16,1,2048]{2,1,0:T(2,128)(2,1)S(1)} %broadcast_in_dim_reshape.5.mask_ref.ma_ref.mk_ref, ...), custom_call_target="tpu_custom_call" | custom-call | flops 4194304 | bytes 6291456 | tf_op jit(solution)/shard_map/coulomb/pallas_call | solution.py:95
  153.5 1.0 copy-done.4
  154.5 0.5 collective-permute-start.9
  155.0 0.1 pad_add_fusion.1.place_ref
  155.0 3.2 coulomb.5
  158.3 0.1 collective-permute-start.7
  158.4 3.2 coulomb.4
  161.6 0.6 collective-permute-start.6
  162.2 0.4 add_convert_fusion
  162.6 1.8 collective-permute-start.12
  164.3 1.6 add_convert_fusion.1
  166.0 0.1 collective-permute-start.10
  166.1 0.4 add_convert_fusion.2
  166.5 0.0 copy-start.7
  166.5 1.0 collective-permute-start.8
  167.5 0.4 add_convert_fusion.3.refs_0_
  167.9 23.7 %collective-permute-done.12.refs_3_ = bf16[256,2048]{1,0:T(8,128)(2,1)S(1)} collective-permute-done((bf16[256,2048]{1,0:T(8,128)(2,1)S(1)}, bf16[256,2048]{1,0:T(8,128)(2,1)S(1)}, u32[]{:S(2)}, u32[]{:S(2)}) %collective-permute-start.12) | collective-permute-done | bytes 1048608 | tf_op jit(solution)/shard_map/ppermute | solution.py:279
  191.6 102.1 %collective-permute-done.10.refs_2_ = bf16[256,2048]{1,0:T(8,128)(2,1)} collective-permute-done((bf16[256,2048]{1,0:T(8,128)(2,1)S(1)}, bf16[256,2048]{1,0:T(8,128)(2,1)}, u32[]{:S(2)}, u32[]{:S(2)}) %collective-permute-start.10) | collective-permute-done | bytes 1048608 | tf_op jit(solution)/shard_map/ppermute | solution.py:279
  293.7 34.7 %all-gather.2.cloned.1.call-done.all_ref = bf16[2,8192,256]{2,1,0:T(8,128)(2,1)} async-done(((bf16[2,512,256]{2,1,0:T(8,128)(2,1)}), bf16[2,8192,256]{2,1,0:T(8,128)(2,1)}) %all-gather.2.cloned.1.call-update) | async-done | bytes 8388624 | tf_op jit(solution)/shard_map/all_gather | solution.py:272
  328.4 0.1 collective-permute-start.13
  328.5 0.5 collective-permute-start.5
  328.9 0.1 collective-permute-start.14
  329.0 0.5 collective-permute-start.15
  329.4 0.1 collective-permute-start.16
  329.5 6.1 %collective-permute-done.5.mate_ref = bf16[2,512,256]{2,1,0:T(8,128)(2,1)S(1)} collective-permute-done((bf16[2,512,256]{2,1,0:T(8,128)(2,1)S(1)}, bf16[2,512,256]{2,1,0:T(8,128)(2,1)S(1)}, u32[]{:S(2)}, u32[]{:S(2)}) %collective-permute-start.5) | collective-permute-done | bytes 524320 | tf_op jit(solution)/shard_map/ppermute | solution.py:189
  335.6 0.4 collective-permute-start.17
  336.0 0.1 pad_add_fusion.place_ref
  336.0 0.2 fusion.9
  336.2 2.5 fusion.3
  338.7 0.1 dynamic_slice.32
  338.8 0.1 copy.42.field_ref
  339.0 8.2 %collective-permute-done.15.refs_5_ = bf16[256,2048]{1,0:T(8,128)(2,1)} collective-permute-done((bf16[256,2048]{1,0:T(8,128)(2,1)}, bf16[256,2048]{1,0:T(8,128)(2,1)}, u32[]{:S(2)}, u32[]{:S(2)}) %collective-permute-start.15) | collective-permute-done | bytes 1048608 | tf_op jit(solution)/shard_map/ppermute | solution.py:189
  347.1 1.5 collective-permute-done.16.refs_6_
  348.7 20.4 %fock.1 = f32[512,8192]{1,0:T(8,128)} custom-call(s32[3]{0:T(128)S(1)} %pad_add_fusion.place_ref, bf16[2,512,256]{2,1,0:T(8,128)(2,1)S(1)} %copy-done.3, bf16[2,512,256]{2,1,0:T(8,128)(2,1)S(1)} %collective-permute-done.5.mate_ref, bf16[2,8192,256]{2,1,0:T(8,128)(2,1)} %all-gather.2.cloned.1.call-done.all_ref, ...), custom_call_target="tpu_custom_call" | custom-call | flops 8589934592 | bytes 41943040 | tf_op jit(solution)/shard_map/fock/pallas_call | solution.py:164
  (36 shorter events, 0.1 us)
Async XLA Ops:
  7.2 51.0 %copy-start = (f32[1024]{0:T(1024)S(1)}, f32[1024]{0:T(1024)}, u32[]{:S(2)}) copy-start(f32[1024]{0:T(1024)} %param.14) | copy-start | bytes 12292
  7.2 50.6 %copy-start.8 = (f32[3,1024]{1,0:T(4,128)S(1)}, f32[3,1024]{1,0:T(4,128)}, u32[]{:S(2)}) copy-start(f32[3,1024]{1,0:T(4,128)} %param.13) | copy-start | bytes 36868
  7.2 321.2 %all-gather.2.cloned.1.call-start = ((), (), s32[]{:S(2)}) async-start(), calls=%async_computation | async-start | bytes 8912896 | tf_op jit(solution)/shard_map/all_gather | solution.py:272
  8.3 3.5 collective-permute-start
  11.8 47.3 %collective-permute-start.1 = (bf16[1024,256]{1,0:T(8,128)(2,1)S(1)}, bf16[1024,256]{1,0:T(8,128)(2,1)S(1)}, u32[]{:S(2)}, u32[]{:S(2)}) collective-permute-start(bf16[1024,256]{1,0:T(8,128)(2,1)S(1)} %collective-permute-done), channel_id=1, source_target_pairs={{0,16},{16,0},{1,17},{17,1},{2,18},{18,2},{3,19},{19,3},{4,20},{20... | collective-permute-start | bytes 1572872 | tf_op jit(solution)/shard_map/ppermute | solution.py:189
  57.8 1.6 copy-start.2
  58.2 1.0 copy-start.6
  74.1 5.1 %copy-start.9 = (s32[1,2]{1,0:T(1,128)S(1)}, s32[1,2]{1,0:T(1,128)}, u32[]{:S(2)}) copy-start(s32[1,2]{1,0:T(1,128)} %param.15) | copy-start | bytes 28
  75.0 68.7 %collective-permute-start.4 = (bf16[2,512,256]{2,1,0:T(8,128)(2,1)}, bf16[2,512,256]{2,1,0:T(8,128)(2,1)}, u32[]{:S(2)}, u32[]{:S(2)}) collective-permute-start(bf16[2,512,256]{2,1,0:T(8,128)(2,1)} %get-tuple-element.44), channel_id=1, source_target_pairs={{0,3},{1,0},{2,1},{3,2},{4,7},{5,4},{6,5},{7,6},{8,11},{9,8},{10,9... | collective-permute-start | bytes 1572872 | tf_op jit(solution)/shard_map/ppermute | solution.py:263
  78.7 65.1 %collective-permute-start.3 = (bf16[2,512,256]{2,1,0:T(8,128)(2,1)S(1)}, bf16[2,512,256]{2,1,0:T(8,128)(2,1)}, u32[]{:S(2)}, u32[]{:S(2)}) collective-permute-start(bf16[2,512,256]{2,1,0:T(8,128)(2,1)S(1)} %get-tuple-element.45), channel_id=1, source_target_pairs={{0,2},{1,3},{2,0},{3,1},{4,6},{5,7},{6,4},{7,5},{8,10},{9,11},{10,... | collective-permute-start | bytes 1572872 | tf_op jit(solution)/shard_map/ppermute | solution.py:263
  78.7 65.1 %collective-permute-start.2 = (bf16[2,512,256]{2,1,0:T(8,128)(2,1)S(1)}, bf16[2,512,256]{2,1,0:T(8,128)(2,1)}, u32[]{:S(2)}, u32[]{:S(2)}) collective-permute-start(bf16[2,512,256]{2,1,0:T(8,128)(2,1)S(1)} %get-tuple-element.46), channel_id=1, source_target_pairs={{0,1},{1,2},{2,3},{3,0},{4,5},{5,6},{6,7},{7,4},{8,9},{9,10},{10,1... | collective-permute-start | bytes 1572872 | tf_op jit(solution)/shard_map/ppermute | solution.py:263
  149.5 12.6 %collective-permute-start.11 = (bf16[256,2048]{1,0:T(8,128)(2,1)S(1)}, bf16[256,2048]{1,0:T(8,128)(2,1)S(1)}, u32[]{:S(2)}, u32[]{:S(2)}) collective-permute-start(bf16[256,2048]{1,0:T(8,128)(2,1)S(1)} %get-tuple-element.37), channel_id=1, source_target_pairs={{0,16},{16,0},{1,17},{17,1},{2,18},{18,2},{3,19},{19,3},{4,20},{20... | collective-permute-start | bytes 3145736 | tf_op jit(solution)/shard_map/ppermute | solution.py:189
  153.5 1.0 copy-start.4
  154.5 9.9 %collective-permute-start.9 = (bf16[256,2048]{1,0:T(8,128)(2,1)}, bf16[256,2048]{1,0:T(8,128)(2,1)}, u32[]{:S(2)}, u32[]{:S(2)}) collective-permute-start(bf16[256,2048]{1,0:T(8,128)(2,1)} %get-tuple-element.35), channel_id=1, source_target_pairs={{0,16},{16,0},{1,17},{17,1},{2,18},{18,2},{3,19},{19,3},{4,20},{20... | collective-permute-start | bytes 3145736 | tf_op jit(solution)/shard_map/ppermute | solution.py:189
  158.3 7.8 %collective-permute-start.7 = (bf16[256,2048]{1,0:T(8,128)(2,1)S(1)}, bf16[256,2048]{1,0:T(8,128)(2,1)S(1)}, u32[]{:S(2)}, u32[]{:S(2)}) collective-permute-start(bf16[256,2048]{1,0:T(8,128)(2,1)S(1)} %get-tuple-element.33), channel_id=1, source_target_pairs={{0,16},{16,0},{1,17},{17,1},{2,18},{18,2},{3,19},{19,3},{4,20},{20... | collective-permute-start | bytes 3145736 | tf_op jit(solution)/shard_map/ppermute | solution.py:189
  161.6 2.7 copy-start.5
  161.6 5.8 %collective-permute-start.6 = (bf16[256,2048]{1,0:T(8,128)(2,1)S(1)}, bf16[256,2048]{1,0:T(8,128)(2,1)S(1)}, u32[]{:S(2)}, u32[]{:S(2)}) collective-permute-start(bf16[256,2048]{1,0:T(8,128)(2,1)S(1)} %get-tuple-element.31), channel_id=1, source_target_pairs={{0,16},{16,0},{1,17},{17,1},{2,18},{18,2},{3,19},{19,3},{4,20},{20... | collective-permute-start | bytes 3145736 | tf_op jit(solution)/shard_map/ppermute | solution.py:189
  162.6 29.0 %collective-permute-start.12 = (bf16[256,2048]{1,0:T(8,128)(2,1)S(1)}, bf16[256,2048]{1,0:T(8,128)(2,1)S(1)}, u32[]{:S(2)}, u32[]{:S(2)}) collective-permute-start(bf16[256,2048]{1,0:T(8,128)(2,1)S(1)} %add_convert_fusion), channel_id=1, source_target_pairs={{0,3},{1,0},{2,1},{3,2},{4,7},{5,4},{6,5},{7,6},{8,11},{9,8},{10,9... | collective-permute-start | bytes 3145736 | tf_op jit(solution)/shard_map/ppermute | solution.py:279
  166.0 127.7 %collective-permute-start.10 = (bf16[256,2048]{1,0:T(8,128)(2,1)S(1)}, bf16[256,2048]{1,0:T(8,128)(2,1)}, u32[]{:S(2)}, u32[]{:S(2)}) collective-permute-start(bf16[256,2048]{1,0:T(8,128)(2,1)S(1)} %add_convert_fusion.1), channel_id=1, source_target_pairs={{0,2},{1,3},{2,0},{3,1},{4,6},{5,7},{6,4},{7,5},{8,10},{9,11},{10,... | collective-permute-start | bytes 3145736 | tf_op jit(solution)/shard_map/ppermute | solution.py:279
  166.5 162.0 %copy-start.3 = (bf16[2,512,256]{2,1,0:T(8,128)(2,1)S(1)}, bf16[2,512,256]{2,1,0:T(8,128)(2,1)}, u32[]{:S(2)}) copy-start(bf16[2,512,256]{2,1,0:T(8,128)(2,1)} %fusion.2.own_ref) | copy-start | bytes 1572868
  166.5 169.6 %copy-start.7 = (f32[8192]{0:T(1024)S(1)}, f32[8192]{0:T(1024)}, u32[]{:S(2)}) copy-start(f32[8192]{0:T(1024)} %param.11) | copy-start | bytes 98308
  166.5 127.2 %collective-permute-start.8 = (bf16[256,2048]{1,0:T(8,128)(2,1)S(1)}, bf16[256,2048]{1,0:T(8,128)(2,1)}, u32[]{:S(2)}, u32[]{:S(2)}) collective-permute-start(bf16[256,2048]{1,0:T(8,128)(2,1)S(1)} %add_convert_fusion.2), channel_id=1, source_target_pairs={{0,1},{1,2},{2,3},{3,0},{4,5},{5,6},{6,7},{7,4},{8,9},{9,10},{10,1... | collective-permute-start | bytes 3145736 | tf_op jit(solution)/shard_map/ppermute | solution.py:279
  328.4 20.3 %collective-permute-start.13 = (bf16[2,8192,256]{2,1,0:T(8,128)(2,1)}, bf16[2,8192,256]{2,1,0:T(8,128)(2,1)}, u32[]{:S(2)}, u32[]{:S(2)}) collective-permute-start(bf16[2,8192,256]{2,1,0:T(8,128)(2,1)} %all-gather.2.cloned.1.call-done.all_ref), channel_id=1, source_target_pairs={{0,16},{16,0},{1,17},{17,1},{2,18},{18,2},{3,19},{19,3},{4,20},{20... | collective-permute-start | bytes 25165832 | tf_op jit(solution)/shard_map/ppermute | solution.py:189
  328.5 7.1 %collective-permute-start.5 = (bf16[2,512,256]{2,1,0:T(8,128)(2,1)S(1)}, bf16[2,512,256]{2,1,0:T(8,128)(2,1)S(1)}, u32[]{:S(2)}, u32[]{:S(2)}) collective-permute-start(bf16[2,512,256]{2,1,0:T(8,128)(2,1)S(1)} %copy-done.3), channel_id=1, source_target_pairs={{0,16},{16,0},{1,17},{17,1},{2,18},{18,2},{3,19},{19,3},{4,20},{20... | collective-permute-start | bytes 1572872 | tf_op jit(solution)/shard_map/ppermute | solution.py:189
  328.9 10.0 %collective-permute-start.14 = (bf16[256,2048]{1,0:T(8,128)(2,1)S(1)}, bf16[256,2048]{1,0:T(8,128)(2,1)}, u32[]{:S(2)}, u32[]{:S(2)}) collective-permute-start(bf16[256,2048]{1,0:T(8,128)(2,1)S(1)} %add_convert_fusion.3.refs_0_), channel_id=1, source_target_pairs={{0,16},{16,0},{1,17},{17,1},{2,18},{18,2},{3,19},{19,3},{4,20},{20... | collective-permute-start | bytes 3145736 | tf_op jit(solution)/shard_map/ppermute | solution.py:189
  329.0 18.2 %collective-permute-start.15 = (bf16[256,2048]{1,0:T(8,128)(2,1)}, bf16[256,2048]{1,0:T(8,128)(2,1)}, u32[]{:S(2)}, u32[]{:S(2)}) collective-permute-start(bf16[256,2048]{1,0:T(8,128)(2,1)} %collective-permute-done.8.refs_1_), channel_id=1, source_target_pairs={{0,16},{16,0},{1,17},{17,1},{2,18},{18,2},{3,19},{19,3},{4,20},{20... | collective-permute-start | bytes 3145736 | tf_op jit(solution)/shard_map/ppermute | solution.py:189
  329.4 19.2 %collective-permute-start.16 = (bf16[256,2048]{1,0:T(8,128)(2,1)}, bf16[256,2048]{1,0:T(8,128)(2,1)}, u32[]{:S(2)}, u32[]{:S(2)}) collective-permute-start(bf16[256,2048]{1,0:T(8,128)(2,1)} %collective-permute-done.10.refs_2_), channel_id=1, source_target_pairs={{0,16},{16,0},{1,17},{17,1},{2,18},{18,2},{3,19},{19,3},{4,20},{20... | collective-permute-start | bytes 3145736 | tf_op jit(solution)/shard_map/ppermute | solution.py:189
  335.6 13.1 %collective-permute-start.17 = (bf16[256,2048]{1,0:T(8,128)(2,1)S(1)}, bf16[256,2048]{1,0:T(8,128)(2,1)}, u32[]{:S(2)}, u32[]{:S(2)}) collective-permute-start(bf16[256,2048]{1,0:T(8,128)(2,1)S(1)} %collective-permute-done.12.refs_3_), channel_id=1, source_target_pairs={{0,16},{16,0},{1,17},{17,1},{2,18},{18,2},{3,19},{19,3},{4,20},{20... | collective-permute-start | bytes 3145736 | tf_op jit(solution)/shard_map/ppermute | solution.py:189
  348.7 20.4 %copy-start.1 = (f32[1024]{0:T(1024)S(1)}, f32[1024]{0:T(1024)}, u32[]{:S(2)}) copy-start(f32[1024]{0:T(1024)} %param.14) | copy-start | bytes 12292
Sparse Core Ops, SparseCore 0:
  146.3 182.0 all-gather.1
